TPU v7x, 256 devices: a whole 4x4x8 slice. The times are simulated.
256 devices in a mesh: seq: 2 (over core), row: 32 (over z, x), col: 4 (over y).
Axes of the slice: x: 4, y: 4, z: 8, core: 2. Of those that a mesh axis runs over, the one named last changes fastest.
Arguments:
- tokens: bfloat16 [8192, 8192], P(('seq', 'row'), 'col'), as said below
- positions: int32 [8192], replicated, may hold values from 0 to 6143, as said below
- w_query: bfloat16 [8192, 8192], P('row', 'col'), as said below
- w_key: bfloat16 [8192, 1024], P(None, 'col'), as said below
- w_value: bfloat16 [8192, 1024], P(None, 'col'), may hold values from -0.125 to 0.125
Outputs:
- context: bfloat16 [8192, 8192], P(('seq', 'row'), 'col')
Inputs may be any that keep to these rules, and one draw needn't show every extreme that they name: positions[i] is 0 at a document's first token and positions[i - 1] + 1 otherwise; the sequence holds at most four documents. `tokens`: real-valued hidden states of order one. `w_query`: real-valued weights. `w_key`: real-valued weights.
All inputs are finite; a program needn't handle non-finite values.
Results may differ from a plain program's by a relative error of at most 0.0085.
Values may be sent and summed in bfloat16 or wider, within the bound.
A program may use at most 128 MiB of HBM per device.

v0:
```python
import math

import jax
import jax.numpy as jnp
from jax import lax
from jax.sharding import PartitionSpec as P

HEADS = 64
KVH = 8
HD = 128


def local(tokens, positions, w_query, w_key, w_value):
    tok_rows = tokens.shape[0]
    half_rows = tok_rows // 2
    group_size = HEADS // KVH
    kv_local = w_key.shape[1] // HD
    score_scale = 1.0 / math.sqrt(HD)
    whole_tokens = lax.all_gather(tokens, "col", axis=1, tiled=True)
    proj_query = jnp.dot(
        whole_tokens,
        lax.all_gather(w_query, "row", axis=0, tiled=True),
        preferred_element_type=jnp.float32,
    )
    query_rows = proj_query.astype(jnp.bfloat16)
    key_rows = jnp.dot(whole_tokens, w_key, preferred_element_type=jnp.float32).astype(jnp.bfloat16)
    value_rows = jnp.dot(whole_tokens, w_value, preferred_element_type=jnp.float32).astype(
        jnp.bfloat16
    )
    my_index = lax.axis_index(("seq", "row"))
    own_base = my_index * tok_rows
    far_rows = query_rows[half_rows:]
    second_base = own_base + half_rows
    query_sets = []
    for rows_part, base_row in ((query_rows[:half_rows], own_base), (far_rows, second_base)):
        query_index = base_row + jnp.arange(half_rows, dtype=jnp.int32)
        doc_start = query_index - lax.dynamic_slice_in_dim(positions, base_row, half_rows, 0)
        arranged = rows_part.reshape(half_rows, kv_local, group_size, HD).transpose(1, 2, 0, 3)
        arranged = arranged.reshape(kv_local, group_size * half_rows, HD)
        query_sets.append((arranged, query_index, doc_start))

    def attend(softmax_state, query_set, key_block, value_block, first_row):
        arranged, query_index, doc_start = query_set
        block_len = key_block.shape[0]
        key_index = jnp.arange(block_len, dtype=jnp.int32)

        def work(running):
            run_max, run_sum, run_acc = running
            key_heads = key_block.reshape(block_len, kv_local, HD).transpose(1, 0, 2)
            value_heads = value_block.reshape(block_len, kv_local, HD).transpose(1, 0, 2)
            scores = (
                jnp.einsum("gqd,gkd->gqk", arranged, key_heads, preferred_element_type=jnp.float32)
                * score_scale
            )
            allowed = (key_index[None, :] <= query_index[:, None]) & (
                key_index[None, :] >= doc_start[:, None]
            )
            allowed = jnp.tile(allowed, (group_size, 1))[None]
            scores = jnp.where(allowed, scores, -1e30)
            new_max = jnp.maximum(run_max, jnp.max(scores, axis=-1, keepdims=True))
            exponent = jnp.where(allowed, jnp.exp(scores - new_max), 0.0)
            new_sum = jnp.sum(exponent, axis=-1, keepdims=True)
            new_acc = jnp.einsum(
                "gqk,gkd->gqd",
                exponent.astype(jnp.bfloat16),
                value_heads,
                preferred_element_type=jnp.float32,
            )
            return (new_max, new_sum, new_acc)

        skipped = (first_row > query_index[-1]) | (first_row + block_len - 1 < jnp.min(doc_start))
        return lax.cond(skipped, lambda running: running, work, softmax_state)

    stacked_rows = group_size * half_rows
    empty_state = (
        jnp.full((kv_local, stacked_rows, 1), -1e30, jnp.float32),
        jnp.zeros((kv_local, stacked_rows, 1), jnp.float32),
        jnp.zeros((kv_local, stacked_rows, HD), jnp.float32),
    )
    initial_states = (empty_state, empty_state)
    pieces = (
        lax.all_gather(key_rows, ("seq", "row"), axis=0, tiled=True),
        lax.all_gather(value_rows, ("seq", "row"), axis=0, tiled=True),
    )
    first_row = jnp.int32(0)
    final_states = tuple(
        (
            attend(one_state, one_set, pieces[0], pieces[1], first_row)
            for one_state, one_set in zip(initial_states, query_sets)
        )
    )

    def finish(one_state):
        run_max, run_sum, run_acc = one_state
        result = (
            (run_acc / run_sum).reshape(kv_local, group_size, half_rows, HD).transpose(2, 0, 1, 3)
        )
        return result.reshape(half_rows, kv_local * group_size * HD).astype(jnp.bfloat16)

    first_out = finish(final_states[0])
    second_out = finish(final_states[1])
    return jnp.concatenate([first_out, second_out], axis=0)


def solution(mesh):
    in_specs = (P(("seq", "row"), "col"), P(), P("row", "col"), P(None, "col"), P(None, "col"))
    out_specs = P(("seq", "row"), "col")
    return jax.shard_map(local, mesh=mesh, in_specs=in_specs, out_specs=out_specs, check_vma=False)
```

profile of v0, /device:TPU:1, one launch (start us, length us, event | category | flops | bytes accessed | tf_op | source)
XLA Modules:
  0.0 561.8 jit_solution(1435217280489886916)
XLA Ops:
  6.5 0.7 all-gather.5.cloned.1.call-update
  7.3 0.7 all-gather.7.cloned.1.call-update
  8.1 38.4 %all-gather.5.cloned.1.call-done = bf16[128,8192]{1,0:T(8,128)(2,1)} async-done(((bf16[128,2048]{1,0:T(8,128)(2,1)}), bf16[128,8192]{1,0:T(8,128)(2,1)}) %all-gather.5.cloned.1.call-update) | async-done | bytes 2097168 | tf_op jit(solution)/shard_map/all_gather | solution.py:19
  46.4 4.3 convolution_convert_fusion.1
  50.8 4.2 convolution_convert_fusion.2
  55.0 1.5 fusion.24
  56.5 0.7 slice.12
  59.1 0.6 slice.14
  60.3 221.6 %all-gather.7.cloned.1.call-done = bf16[8192,2048]{1,0:T(8,128)(2,1)} async-done(((bf16[256,2048]{1,0:T(8,128)(2,1)}), bf16[8192,2048]{1,0:T(8,128)(2,1)}) %all-gather.7.cloned.1.call-update) | async-done | bytes 33554448 | tf_op jit(solution)/shard_map/all_gather | solution.py:22
  281.9 13.0 %convolution_convert_fusion = bf16[128,2048]{1,0:T(8,128)(2,1)S(1)} fusion(bf16[128,8192]{1,0:T(8,128)(2,1)S(1)} %copy-done, bf16[8192,2048]{1,0:T(8,128)(2,1)} %all-gather.7.cloned.1.call-done), kind=kOutput, calls=%fused_computation.34 | convolution fusion | flops 4295229440 | bytes 36175872 | tf_op jit(solution)/shard_map/dot_general | solution.py:20
  295.1 66.5 %all-gather.11.cloned.1.call-done = bf16[8192,256]{1,0:T(8,128)(2,1)} async-done(((bf16[128,256]{1,0:T(8,128)(2,1)}), bf16[8192,256]{1,0:T(8,128)(2,1)}) %all-gather.11.cloned.1.call-update) | async-done | bytes 4194320 | tf_op jit(solution)/shard_map/all_gather | solution.py:83
  361.5 78.9 %all-gather.9.cloned.1.call-done = bf16[8192,256]{1,0:T(8,128)(2,1)} async-done(((bf16[128,256]{1,0:T(8,128)(2,1)}), bf16[8192,256]{1,0:T(8,128)(2,1)}) %all-gather.9.cloned.1.call-update) | async-done | bytes 4194320 | tf_op jit(solution)/shard_map/all_gather | solution.py:82
  440.4 56.3 %conditional.2 = (f32[2,512,1]{1,0,2:T(2,128)S(1)}, f32[2,512,128]{2,1,0:T(8,128)S(1)}) conditional(s32[]{:T(128)} %convert_element_type.45, (s32[8192]{0:T(1024)S(1)}, s32[8192]{0:T(1024)S(1)}, s32[64]{0:T(128)S(1)}, s32[64]{0:T(128)S(1)}, bf16[2,8,64,128]{3,2,1,0:T(8,128)(2,1)S(1)}, /*index=5*/bf16[8192,256]{1,0:T(8,128)(2,1)}, ...), branch_computations={%region_1.4_spmd, %region_4.5_spmd} | conditional | flops 4405591040 | bytes 144532016 | solution.py:72
  440.9 3.9 tile.4
  444.8 17.6 %fusion = (f32[2,512]{1,0:T(2,128)S(1)}, f32[2,512,8192]{2,1,0:T(8,128)}) fusion(pred[512,8192]{1,0:T(8,128)(4,1)} %bitcast.94, bf16[2,512,128]{2,1,0:T(8,128)(2,1)S(1)} %bitcast.109, bf16[8192,256]{1,0:T(8,128)(2,1)} %get-tuple-element.38), kind=kOutput, calls=%fused_computation.2 | convolution fusion | flops 2172648448 | bytes 42209280 | tf_op jit(solution)/shard_map/cond/branch_0_fun/gqd,gkd->gqk/dot_general | solution.py:52
  462.4 18.3 %fusion.3 = f32[2,512,128]{2,1,0:T(8,128)S(1)} fusion(f32[2,512,8192]{2,1,0:T(8,128)} %get-tuple-element.60, f32[2,512]{1,0:T(2,128)S(1)} %broadcast_maximum_fusion, pred[512,8192]{1,0:T(8,128)(4,1)} %bitcast.95, bf16[8192,256]{1,0:T(8,128)(2,1)} %get-tuple-element.39), kind=kOutput, calls=%fused_computation.5 | convolution fusion | flops 2189426688 | bytes 42471424 | tf_op jit(solution)/shard_map/cond/branch_0_fun/gqk,gkd->gqd/dot_general | solution.py:63
  480.8 16.0 %fusion.2 = f32[2,512]{1,0:T(2,128)S(1)} fusion(f32[2,512,8192]{2,1,0:T(8,128)} %get-tuple-element.60, f32[2,512]{1,0:T(2,128)S(1)} %broadcast_maximum_fusion, pred[512,8192]{1,0:T(8,128)(4,1)S(1)} %bitcast.96), kind=kLoop, calls=%fused_computation.4 | loop fusion | flops 41942016 | bytes 37756928 | tf_op jit(solution)/shard_map/cond/branch_0_fun/reduce_sum | solution.py:62
  497.4 56.6 %conditional.3 = (f32[2,512,1]{1,0,2:T(2,128)S(1)}, f32[2,512,128]{2,1,0:T(8,128)S(1)}) conditional(s32[]{:T(128)} %convert_element_type.53, (s32[8192]{0:T(1024)S(1)}, s32[8192]{0:T(1024)S(1)}, s32[64]{0:T(128)S(1)}, s32[64]{0:T(128)S(1)}, bf16[2,8,64,128]{3,2,1,0:T(8,128)(2,1)S(1)}, /*index=5*/bf16[8192,256]{1,0:T(8,128)(2,1)}, ...), branch_computations={%region_6.9_spmd, %region_9.10_spmd} | conditional | flops 4405591040 | bytes 144532016 | solution.py:72
  497.6 0.5 compare_and_fusion.1
  498.1 3.9 tile.11
  502.0 17.6 %fusion.12 = (f32[2,512]{1,0:T(2,128)S(1)}, f32[2,512,8192]{2,1,0:T(8,128)}) fusion(pred[512,8192]{1,0:T(8,128)(4,1)} %bitcast.97, bf16[2,512,128]{2,1,0:T(8,128)(2,1)S(1)} %bitcast.111, bf16[8192,256]{1,0:T(8,128)(2,1)} %get-tuple-element.45), kind=kOutput, calls=%fused_computation.19 | convolution fusion | flops 2172648448 | bytes 42209280 | tf_op jit(solution)/shard_map/cond/branch_0_fun/gqd,gkd->gqk/dot_general | solution.py:52
  519.6 18.3 %fusion.15 = f32[2,512,128]{2,1,0:T(8,128)S(1)} fusion(f32[2,512,8192]{2,1,0:T(8,128)} %get-tuple-element.62, f32[2,512]{1,0:T(2,128)S(1)} %broadcast_maximum_fusion.1, pred[512,8192]{1,0:T(8,128)(4,1)} %bitcast.98, bf16[8192,256]{1,0:T(8,128)(2,1)} %get-tuple-element.46), kind=kOutput, calls=%fused_computation.22 | convolution fusion | flops 2189426688 | bytes 42471424 | tf_op jit(solution)/shard_map/cond/branch_0_fun/gqk,gkd->gqd/dot_general | solution.py:63
  538.0 16.0 %fusion.14 = f32[2,512]{1,0:T(2,128)S(1)} fusion(f32[2,512,8192]{2,1,0:T(8,128)} %get-tuple-element.62, f32[2,512]{1,0:T(2,128)S(1)} %broadcast_maximum_fusion.1, pred[512,8192]{1,0:T(8,128)(4,1)S(1)} %bitcast.99), kind=kLoop, calls=%fused_computation.21 | loop fusion | flops 41942016 | bytes 37756928 | tf_op jit(solution)/shard_map/cond/branch_0_fun/reduce_sum | solution.py:62
  554.5 0.8 pad_maximum_fusion
  (29 shorter events, 1.8 us)
Async XLA Ops:
  6.5 39.9 %all-gather.5.cloned.1.call-start = ((), (), s32[]{:S(2)}) async-start(), calls=%async_computation | async-start | bytes 2621440 | tf_op jit(solution)/shard_map/all_gather | solution.py:19
  7.3 274.7 %all-gather.7.cloned.1.call-start = ((), (), s32[]{:S(2)}) async-start(), calls=%async_computation.1 | async-start | bytes 34603008 | tf_op jit(solution)/shard_map/all_gather | solution.py:22
  8.0 353.5 %all-gather.11.cloned.1.call-start = ((), (), s32[]{:S(2)}) async-start(), calls=%async_computation.3 | async-start | bytes 4259840 | tf_op jit(solution)/shard_map/all_gather | solution.py:83
  46.4 235.5 %copy-start = (bf16[128,8192]{1,0:T(8,128)(2,1)S(1)}, bf16[128,8192]{1,0:T(8,128)(2,1)}, u32[]{:S(2)}) copy-start(bf16[128,8192]{1,0:T(8,128)(2,1)} %all-gather.5.cloned.1.call-done) | copy-start | bytes 6291460
  50.7 389.7 %all-gather.9.cloned.1.call-start = ((), (), s32[]{:S(2)}) async-start(), calls=%async_computation.2 | async-start | bytes 4259840 | tf_op jit(solution)/shard_map/all_gather | solution.py:82
  462.4 18.3 %copy-start.1 = (pred[8,64,8192]{2,1,0:T(8,128)(4,1)S(1)}, pred[8,64,8192]{2,1,0:T(8,128)(4,1)}, u32[]{:S(2)}) copy-start(pred[8,64,8192]{2,1,0:T(8,128)(4,1)} %tile.4) | copy-start | bytes 12582916 | tf_op jit(solution)/shard_map/cond
  519.6 18.3 %copy-start.2 = (pred[8,64,8192]{2,1,0:T(8,128)(4,1)S(1)}, pred[8,64,8192]{2,1,0:T(8,128)(4,1)}, u32[]{:S(2)}) copy-start(pred[8,64,8192]{2,1,0:T(8,128)(4,1)} %tile.11) | copy-start | bytes 12582916 | tf_op jit(solution)/shard_map/cond
Sparse Core Ops, SparseCore 0:
  9.2 37.2 all-gather.4
  49.0 232.8 all-gather.6
  284.7 76.7 all-gather.10
  364.2 76.1 all-gather.8
where the time goes:
time: 562 us
  waiting for transfers between devices  407 us (72%)
  matrix products  93.3 us (17%)
  other arithmetic  35.7 us (6%)
  between operations  15.8 us (3%)
  local copies, waits for them, and re-layouts  9.92 us (2%)
    all_gather x1, waiting for transfers between devices, local(): lax.all_gather(w_query, 'row', axis=0, tiled=True)  222 us
    all_gather x1, waiting for transfers between devices, local(): lax.all_gather(key_rows, ('seq', 'row'), axis=0, tiled=True)  78.9 us
    all_gather x1, waiting for transfers between devices, local(): lax.all_gather(value_rows, ('seq', 'row'), axis=0, tiled=True)  66.5 us
    all_gather x1, waiting for transfers between devices, local(): whole_tokens = lax.all_gather(tokens, 'col', axis=1, tiled=True)  38.4 us
    dot_general x2, matrix products, work(): jnp.einsum('gqk,gkd->gqd', exponent.astype(jnp.bfloat16), value_heads, pr...  36.7 us
    dot_general x2, matrix products, work(): jnp.einsum('gqd,gkd->gqk', arranged, key_heads, preferred_element_type=jn...  35.2 us
    reduce_sum x2, other arithmetic, work(): new_sum = jnp.sum(exponent, axis=-1, keepdims=True)  31.9 us
    dot_general x1, matrix products, local(): jnp.dot(whole_tokens, lax.all_gather(w_query, 'row', axis=0, tiled=True),...  13 us
  transfers between devices with their start and end apart: 4, of which 4 were waited for; matrix products, arithmetic and copies ran while one was open for 4% of the time, Pallas kernels for 0%

commit v1 on v0

v1 whole, which is shorter than its diff:
```python
import functools
import math

import jax
import jax.numpy as jnp
from jax import lax
from jax.experimental import pallas as pl
from jax.experimental.pallas import tpu as pltpu
from jax.sharding import PartitionSpec as P

HD = 128
NX, NY, NZ = 4, 4, 8
ROWS = 128
CHUNK = NX * ROWS
MESH = pl.DeviceIdType.MESH
LOG2E = 1.4426950408889634
NEG = -1e30


def place():
    row = lax.axis_index("row")
    return lax.axis_index("seq"), row // NX, row % NX, lax.axis_index("col")


def greet(partners):
    barrier = pltpu.get_barrier_semaphore()
    for partner in partners:
        pl.semaphore_signal(barrier, inc=1, device_id=partner, device_id_type=MESH)
    pl.semaphore_wait(barrier, len(partners))


def project_kernel(
    tok_ref, wq_ref, wk_ref, wv_ref, q_ref, kv_ref, tok, wq, wkv, acc, qsend, loc, ssem, rsem
):
    core, z, x, y = place()
    sib = 1 - core

    def at(dz=0, dx=0, dy=0, c=core):
        return (c, (z + dz) % NZ * NX + (x + dx) % NX, (y + dy) % NY)

    step = {"x+": (0, 1, 0), "x-": (0, -1, 0), "y+": (0, 0, 1), "y-": (0, 0, -1),
            "z+": (1, 0, 0), "z-": (-1, 0, 0)}
    slots = {}
    sent = []

    def slot(key):
        return slots.setdefault(key, len(slots))

    def put(key, src, dst, device):
        i = slot(key)
        copy = pltpu.make_async_remote_copy(
            src_ref=src, dst_ref=dst, send_sem=ssem.at[i], recv_sem=rsem.at[i],
            device_id=device, device_id_type=MESH)
        copy.start()
        sent.append(copy)

    def take(key, dst):
        i = slot(key)
        pltpu.make_async_remote_copy(
            src_ref=dst, dst_ref=dst, send_sem=ssem.at[i], recv_sem=rsem.at[i],
            device_id=at(c=sib), device_id_type=MESH).wait_recv()

    head = x // 2
    my_w = pl.ds(pl.multiple_of(x * 512 + core * 256, 256), 256)
    head_cols = pl.ds(pl.multiple_of(head * HD, HD), HD)
    loads = [
        pltpu.make_async_copy(tok_ref, tok.at[x, y], loc.at[0]),
        pltpu.make_async_copy(wq_ref.at[:, my_w], wq.at[core, z * NX + x], loc.at[1]),
        pltpu.make_async_copy(wk_ref.at[:, head_cols], wkv.at[:, pl.ds(0, HD)], loc.at[2]),
        pltpu.make_async_copy(wv_ref.at[:, head_cols], wkv.at[:, pl.ds(HD, HD)], loc.at[3]),
    ]
    for load in loads:
        load.start()

    greet([at(dx=1), at(dx=2), at(dx=3), at(dy=1), at(dy=3), at(dz=1), at(dz=7), at(c=sib)])

    for dx in (1, 3, 2):
        cols = pl.ds(pl.multiple_of((x + dx) % NX * 512 + core * 256, 256), 256)
        put(("w", dx), wq_ref.at[:, cols], wq.at[core, z * NX + x], at(dx=dx))

    def block(u, v, h, q):
        start, size = (h * 64, 64) if q is None else (h * 64 + q * 32, 32)
        return tok.at[(x + u) % NX, (y + v) % NY, pl.ds(start, size)]

    def orient(h, a, b):
        return (a, b) if h == 0 else (b, a)

    def axis(h, order):
        return ("y", "x")[h] if order == 0 else ("x", "y")[h]

    def token_put(h, order, sign, a, b, q=None):
        d = axis(h, order) + sign
        ref = block(*orient(h, a, b), h, q)
        dz, dx, dy = step[d]
        put((d, h, a, b, q), ref, ref, at(dx=dx, dy=dy))

    def token_take(h, order, sign, a, b, q=None):
        d = axis(h, order) + sign
        move = -1 if sign == "+" else 1
        a2, b2 = (a, b + move) if order == 0 else (a + move, b)
        take((d, h, a, b, q), block(*orient(h, a2, b2), h, q))

    loads[0].wait()
    for h in (0, 1):
        for sign in "+-":
            token_put(h, 0, sign, 0, 0)
    for h in (0, 1):
        for sign in "+-":
            token_put(h, 1, sign, 0, 0)

    def ring_step(name, unit, sign, dist, h):
        way = -1 if sign == "+" else 1
        ref = unit(way * dist, h)
        if dist:
            take((name, sign, dist, h), ref)
        if dist < 3 or (dist == 3 and h == (0 if sign == "+" else 1)):
            dz = step["z" + sign][0]
            put((name, sign, dist + 1, h), ref, ref, at(dz=dz))
        if dist or sign == "+":
            put((name, "c", way * dist, h), ref, ref, at(c=sib))

    def w_unit(dz, h):
        return wq.at[core, pl.ds((z + dz) % NZ * NX + 2 * h, 2)]

    loads[1].wait()
    for dx in (1, 3, 2):
        take(("w", dx), wq.at[core, z * NX + (x - dx) % NX])
    for h in (0, 1):
        for sign in "+-":
            ring_step("W", w_unit, sign, 0, h)

    def w_round(dist, h):
        for sign in "+-":
            ring_step("W", w_unit, sign, dist, h)

    for sign, q in (("+", 0), ("-", 1)):
        for h in (0, 1):
            b = -1 if sign == "+" else 1
            token_take(h, 0, sign, 0, 0)
            token_put(h, 0, sign, 0, b, q)
            for sign2 in "+-":
                token_put(h, 1, sign2, 0, b)
    w_round(1, 0)
    for sign, q in (("+", 0), ("-", 1)):
        for h in (0, 1):
            token_take(h, 1, sign, 0, 0)
            token_put(h, 1, sign, -1 if sign == "+" else 1, 0, q)
    w_round(1, 1)
    for sign, q in (("+", 0), ("-", 1)):
        for h in (0, 1):
            b = -1 if sign == "+" else 1
            token_take(h, 0, sign, 0, b, q)
            for sign2 in "+-":
                token_put(h, 1, sign2, 0, 2 * b, q)
    w_round(2, 0)
    for b in (-1, 1):
        for sign, q in (("+", 0), ("-", 1)):
            for h in (0, 1):
                token_take(h, 1, sign, 0, b)
                token_put(h, 1, sign, -1 if sign == "+" else 1, b, q)
        w_round(2, 1) if b == -1 else w_round(3, 0)
    for sign, q in (("+", 0), ("-", 1)):
        for h in (0, 1):
            b = -2 if sign == "+" else 2
            token_take(h, 1, sign, 0, b, q)
            token_put(h, 1, sign, -1 if sign == "+" else 1, b, q)
    for sign, q in (("+", 1), ("-", 0)):
        for h in (0, 1):
            token_take(h, 1, sign, 0, -2 if q == 0 else 2, q)
    w_round(3, 1)
    for sign, q in (("+", 0), ("-", 1)):
        a = -1 if sign == "+" else 1
        for b in (0, -1, 1, 2 * a):
            for h in (0, 1):
                token_take(h, 1, sign, a, b, q)

    def dot(weights, width):
        acc[:, pl.ds(0, width)] = jnp.zeros((CHUNK, width), jnp.float32)

        def body(j, carry):
            col = pl.multiple_of(j % 2 * 1024, 1024)
            left = tok[:, pl.ds(j // 2, 1), :, pl.ds(col, 1024)].reshape(CHUNK, 1024)
            acc[:, pl.ds(0, width)] += jnp.dot(
                left, weights(j), preferred_element_type=jnp.float32)
            return carry

        lax.fori_loop(0, 8, body, 0)

    loads[2].wait()
    loads[3].wait()
    dot(lambda j: wkv[pl.ds(pl.multiple_of(j * 1024, 1024), 1024), :], 2 * HD)
    kv_ref[pl.ds(core, 1), pl.ds(z, 1)] = (
        acc[:, pl.ds(0, 2 * HD)].astype(jnp.bfloat16).reshape(1, 1, CHUNK, 2 * HD))

    def kv_unit(dz, h):
        return kv_ref.at[core, (z + dz) % NZ, pl.ds(h * 256, 256)]

    def kv_round(dist, h):
        for sign in "+-":
            ring_step("K", kv_unit, sign, dist, h)

    kv_round(0, 0)
    kv_round(0, 1)
    ring_step("W", w_unit, "+", 4, 0)
    ring_step("W", w_unit, "-", 4, 1)
    for dz in (0, -1, 1, -2, 2, -3, 3):
        for h in (0, 1):
            take(("W", "c", dz, h), wq.at[sib, pl.ds((z + dz) % NZ * NX + 2 * h, 2)])
    for dz, h in ((-4, 0), (4, 1)):
        take(("W", "c", dz, h), wq.at[sib, pl.ds((z + dz) % NZ * NX + 2 * h, 2)])

    def q_dot(c):
        dot(lambda j: wq[pl.ds(c, 1), pl.ds(j * 4, 4)].reshape(1024, 256), 256)

    q_dot(sib)
    qsend[...] = acc[:, pl.ds(0, 256)].astype(jnp.bfloat16)
    put(("Q",), qsend, q_ref.at[core], at(c=sib))
    kv_round(1, 0)
    kv_round(1, 1)
    q_dot(core)
    q_ref[pl.ds(core, 1)] = acc[:, pl.ds(0, 256)].astype(jnp.bfloat16).reshape(1, CHUNK, 256)
    for dist in (2, 3):
        kv_round(dist, 0)
        kv_round(dist, 1)
    ring_step("K", kv_unit, "+", 4, 0)
    ring_step("K", kv_unit, "-", 4, 1)
    take(("Q",), q_ref.at[sib])
    for dz in (0, -1, 1, -2, 2, -3, 3):
        for h in (0, 1):
            take(("K", "c", dz, h), kv_ref.at[sib, (z + dz) % NZ, pl.ds(h * 256, 256)])
    for dz, h in ((-4, 0), (4, 1)):
        take(("K", "c", dz, h), kv_ref.at[sib, (z + dz) % NZ, pl.ds(h * 256, 256)])
    for copy in sent:
        copy.wait_send()


COPIES = 128


def project(tokens, w_query, w_key, w_value):
    anywhere = pl.BlockSpec(memory_space=pltpu.HBM)
    return pl.pallas_call(
        project_kernel,
        name="project",
        out_shape=[
            jax.ShapeDtypeStruct((2, CHUNK, 256), jnp.bfloat16),
            jax.ShapeDtypeStruct((2, NZ, CHUNK, 2 * HD), jnp.bfloat16),
        ],
        in_specs=[anywhere] * 4,
        out_specs=[pl.BlockSpec(memory_space=pltpu.VMEM)] * 2,
        scratch_shapes=[
            pltpu.VMEM((NX, NY, ROWS, 2048), jnp.bfloat16),
            pltpu.VMEM((2, NZ * NX, 256, 256), jnp.bfloat16),
            pltpu.VMEM((8192, 2 * HD), jnp.bfloat16),
            pltpu.VMEM((CHUNK, 256), jnp.float32),
            pltpu.VMEM((CHUNK, 256), jnp.bfloat16),
            pltpu.SemaphoreType.DMA((4,)),
            pltpu.SemaphoreType.DMA((COPIES,)),
            pltpu.SemaphoreType.DMA((COPIES,)),
        ],
        compiler_params=pltpu.CompilerParams(
            collective_id=0, has_side_effects=True, vmem_limit_bytes=56 * 2**20),
    )(tokens, w_query, w_key, w_value)


QT = 256
KT = 512


def attend_kernel(pos_s, pos_v, q_ref, kv_ref, o_ref, m_sc, l_sc, acc_sc):
    z = lax.axis_index("row") // NX
    scale = LOG2E / math.sqrt(HD)
    for s in range(2):
        for t in range(CHUNK // QT):
            base = s * (NZ * CHUNK) + z * CHUNK + t * QT
            first_doc = base - pos_s[base]
            last_doc = base + QT - 1 - pos_s[base + QT - 1]
            diag = s * NZ + z
            queries = jnp.concatenate(
                [q_ref[s, t * QT:(t + 1) * QT, :HD], q_ref[s, t * QT:(t + 1) * QT, HD:]], axis=0)
            m_sc[...] = jnp.full_like(m_sc, NEG)
            l_sc[...] = jnp.zeros_like(l_sc)
            acc_sc[...] = jnp.zeros_like(acc_sc)

            def block(kb, masked):
                keys = kv_ref[pl.ds(kb, 1), :, :HD].reshape(KT, HD)
                values = kv_ref[pl.ds(kb, 1), :, HD:].reshape(KT, HD)
                scores = lax.dot_general(
                    queries, keys, (((1,), (1,)), ((), ())), preferred_element_type=jnp.float32)
                if masked:
                    starts = []
                    for r in range(QT // 128):
                        at_row = base // 128 + r
                        pos = pos_v[pl.ds(at_row, 1), :]
                        lane = lax.broadcasted_iota(jnp.int32, (1, 128), 1)
                        begin = at_row * 128 + lane - pos
                        starts.append(jnp.broadcast_to(begin, (128, 128)).T)
                    begin = jnp.concatenate(starts, axis=0)
                    begin = jnp.concatenate([begin] * (KT // 128), axis=1)
                    row = base + lax.broadcasted_iota(jnp.int32, (QT, KT), 0)
                    key = kb * KT + lax.broadcasted_iota(jnp.int32, (QT, KT), 1)
                    allowed = (key <= row) & (key >= begin)
                    allowed = jnp.concatenate([allowed, allowed], axis=0)
                    scores = jnp.where(allowed, scores, NEG)
                old_max = m_sc[...]
                new_max = jnp.maximum(old_max, jnp.max(scores, axis=1, keepdims=True))
                wide_max = jnp.concatenate([new_max] * (KT // 128), axis=1)
                exponent = jnp.exp2((scores - wide_max) * scale)
                if masked:
                    exponent = jnp.where(allowed, exponent, 0.0)
                shrink = jnp.exp2((old_max - new_max) * scale)
                m_sc[...] = new_max
                l_sc[...] = l_sc[...] * shrink + jnp.sum(exponent, axis=1, keepdims=True)
                acc_sc[...] = acc_sc[...] * shrink + jnp.dot(
                    exponent.astype(jnp.bfloat16), values, preferred_element_type=jnp.float32)

            low = first_doc // KT

            def body(kb, carry):
                whole = kb * KT >= last_doc

                @pl.when(whole)
                def _():
                    block(kb, False)

                @pl.when(jnp.logical_not(whole))
                def _():
                    block(kb, True)

                return carry

            lax.fori_loop(low, diag, body, 0)
            block(diag, True)
            result = (acc_sc[...] / l_sc[...]).astype(jnp.bfloat16)
            o_ref[s, t * QT:(t + 1) * QT, :HD] = result[:QT]
            o_ref[s, t * QT:(t + 1) * QT, HD:] = result[QT:]


def attend(positions, q, kv):
    vmem = pl.BlockSpec(memory_space=pltpu.VMEM)
    return pl.pallas_call(
        attend_kernel,
        name="attend",
        out_shape=jax.ShapeDtypeStruct((2, CHUNK, 256), jnp.bfloat16),
        in_specs=[pl.BlockSpec(memory_space=pltpu.SMEM), vmem, vmem, vmem],
        out_specs=vmem,
        scratch_shapes=[
            pltpu.VMEM((2 * QT, 128), jnp.float32),
            pltpu.VMEM((2 * QT, 128), jnp.float32),
            pltpu.VMEM((2 * QT, HD), jnp.float32),
        ],
        compiler_params=pltpu.CompilerParams(vmem_limit_bytes=56 * 2**20),
    )(positions, positions.reshape(64, 128), q, kv.reshape(2 * NZ, CHUNK, 2 * HD))


def spread_kernel(ctx_ref, out_ref, loc, ssem, rsem):
    core, z, x, y = place()
    moves = [(dc, dx) for dx in (2, 1, 3, 0) for dc in (1, 0)][:-1]

    def at(dc, dx):
        return ((core + dc) % 2, z * NX + (x + dx) % NX, y)

    def cols(c, xx):
        return pl.ds(pl.multiple_of(xx * 512 + c * 256, 256), 256)

    def piece(c, xx):
        return ctx_ref.at[c, pl.ds(pl.multiple_of(xx * ROWS, ROWS), ROWS)]

    greet([at(dc, dx) for dc, dx in moves])
    copies = []
    for i, (dc, dx) in enumerate(moves):
        copy = pltpu.make_async_remote_copy(
            src_ref=piece((core + dc) % 2, (x + dx) % NX), dst_ref=out_ref.at[:, cols(core, x)],
            send_sem=ssem.at[i], recv_sem=rsem.at[i], device_id=at(dc, dx), device_id_type=MESH)
        copy.start()
        copies.append(copy)
    own = pltpu.make_async_copy(piece(core, x), out_ref.at[:, cols(core, x)], loc)
    own.start()
    own.wait()
    for copy in copies:
        copy.wait_send()
    for i, (dc, dx) in enumerate(moves):
        land = out_ref.at[:, cols((core + dc) % 2, (x - dx) % NX)]
        pltpu.make_async_remote_copy(
            src_ref=land, dst_ref=land, send_sem=ssem.at[i], recv_sem=rsem.at[i],
            device_id=at(dc, dx), device_id_type=MESH).wait_recv()


def spread(ctx):
    vmem = pl.BlockSpec(memory_space=pltpu.VMEM)
    return pl.pallas_call(
        spread_kernel,
        name="spread",
        out_shape=jax.ShapeDtypeStruct((ROWS, 2048), jnp.bfloat16),
        in_specs=[vmem],
        out_specs=vmem,
        scratch_shapes=[
            pltpu.SemaphoreType.DMA,
            pltpu.SemaphoreType.DMA((7,)),
            pltpu.SemaphoreType.DMA((7,)),
        ],
        compiler_params=pltpu.CompilerParams(collective_id=1, has_side_effects=True),
    )(ctx)


def local(tokens, positions, w_query, w_key, w_value):
    q, kv = project(tokens, w_query, w_key, w_value)
    return spread(attend(positions, q, kv))


def solution(mesh):
    in_specs = (P(("seq", "row"), "col"), P(), P("row", "col"), P(None, "col"), P(None, "col"))
    out_specs = P(("seq", "row"), "col")
    return jax.shard_map(local, mesh=mesh, in_specs=in_specs, out_specs=out_specs, check_vma=False)
```

time: 562 us -> 126 us (0.22)
  the two profiles are of different devices: /device:TPU:1 before, /device:TPU:96 now
where the time goes in v1:
time: 126 us
  Pallas kernels  124 us (98%)
  local copies, waits for them, and re-layouts  1.88 us (1%)
    pallas_call x1, Pallas kernels, project(): pl.pallas_call(project_kernel, name='project', out_shape=[jax.ShapeDtypeS...  88.9 us
    pallas_call x1, Pallas kernels, attend(): pl.pallas_call(attend_kernel, name='attend', out_shape=jax.ShapeDtypeStru...  23 us
    pallas_call x1, Pallas kernels, spread(): pl.pallas_call(spread_kernel, name='spread', out_shape=jax.ShapeDtypeStru...  12 us

profile of v1, /device:TPU:96, one launch (start us, length us, event | category | flops | bytes accessed | tf_op | source)
XLA Modules:
  0.0 125.7 jit_solution(6149015298993964977)
XLA Ops:
  0.0 88.9 %project.1 = (bf16[2,512,256]{2,1,0:T(8,128)(2,1)}, bf16[2,8,512,256]{3,2,1,0:T(8,128)(2,1)}) custom-call(bf16[128,2048]{1,0:T(8,128)(2,1)} %tok_ref.1, bf16[256,2048]{1,0:T(8,128)(2,1)} %wq_ref.1, bf16[8192,256]{1,0:T(8,128)(2,1)} %wk_ref.1, bf16[8192,256]{1,0:T(8,128)(2,1)} %wv_ref.1), custom_call_target="tpu_custom_call" | custom-call | tf_op jit(solution)/shard_map/project/pallas_call | solution.py:242
  88.9 23.0 %attend.1.ctx_ref = bf16[2,512,256]{2,1,0:T(8,128)(2,1)} custom-call(s32[8192]{0:T(1024)} %pos_s.1, s32[64,128]{1,0:T(8,128)} %bitcast.3, bf16[2,512,256]{2,1,0:T(8,128)(2,1)} %get-tuple-element.7.q_ref, bf16[16,512,256]{2,1,0:T(8,128)(2,1)} %bitcast.2), custom_call_target="tpu_custom_call" | custom-call | tf_op jit(solution)/shard_map/attend/pallas_call | solution.py:341
  111.9 12.0 %spread.1 = bf16[128,2048]{1,0:T(8,128)(2,1)} custom-call(bf16[2,512,256]{2,1,0:T(8,128)(2,1)} %attend.1.ctx_ref), custom_call_target="tpu_custom_call" | custom-call | tf_op jit(solution)/shard_map/spread/pallas_call | solution.py:391
  123.9 1.9 %copy.7 = bf16[128,2048]{1,0:T(8,128)(2,1)} copy(bf16[128,2048]{1,0:T(8,128)(2,1)} %spread.1) | data formatting | bytes 1048576

commit v2 on v1

v2 whole, which is shorter than its diff:
```python
import functools
import math

import jax
import jax.numpy as jnp
from jax import lax
from jax.experimental import pallas as pl
from jax.experimental.pallas import tpu as pltpu
from jax.sharding import PartitionSpec as P

HD = 128
NX, NY, NZ = 4, 4, 8
ROWS = 128
CHUNK = NX * ROWS
MESH = pl.DeviceIdType.MESH
LOG2E = 1.4426950408889634
NEG = -1e30


def place():
    row = lax.axis_index("row")
    return lax.axis_index("seq"), row // NX, row % NX, lax.axis_index("col")


def greet(partners):
    barrier = pltpu.get_barrier_semaphore()
    for partner in partners:
        pl.semaphore_signal(barrier, inc=1, device_id=partner, device_id_type=MESH)
    pl.semaphore_wait(barrier, len(partners))


def kernel_body(
    tok_ref, pos_ref, wq_ref, wk_ref, wv_ref, out_ref, tok, wq, wkv, kv, feat, q, qsend, qland, acc,
    docs, top, ctx_acc, ctx, loc, ssem, rsem, ksend, krecv,
    osend, orecv
):
    core, z, x, y = place()
    sib = 1 - core

    def at(dz=0, dx=0, dy=0, c=core):
        return (c, (z + dz) % NZ * NX + (x + dx) % NX, (y + dy) % NY)

    step = {"x+": (0, 1, 0), "x-": (0, -1, 0), "y+": (0, 0, 1), "y-": (0, 0, -1),
            "z+": (1, 0, 0), "z-": (-1, 0, 0)}
    slots = {}
    sent = []

    def slot(key):
        return slots.setdefault(key, len(slots))

    def put(key, src, dst, device):
        i = slot(key)
        copy = pltpu.make_async_remote_copy(
            src_ref=src, dst_ref=dst, send_sem=ssem.at[i], recv_sem=rsem.at[i],
            device_id=device, device_id_type=MESH)
        copy.start()
        sent.append(copy)

    def take(key, dst):
        i = slot(key)
        pltpu.make_async_remote_copy(
            src_ref=dst, dst_ref=dst, send_sem=ssem.at[i], recv_sem=rsem.at[i],
            device_id=at(c=sib), device_id_type=MESH).wait_recv()

    def document_features():
        first = (pos_ref[...] == 0).astype(jnp.bfloat16)
        r = lax.broadcasted_iota(jnp.int32, (HD, HD), 0)
        c = lax.broadcasted_iota(jnp.int32, (HD, HD), 1)
        within = jnp.dot(first, (r <= c).astype(jnp.bfloat16), preferred_element_type=jnp.float32)
        total = jnp.broadcast_to(within[:, HD - 1:], within.shape).astype(jnp.bfloat16)
        before = (c < r).astype(jnp.bfloat16)[:64, :64]
        docs[...] = within + jnp.dot(before, total, preferred_element_type=jnp.float32)

        def body(b, carry):
            for part in range(CHUNK // HD):
                row = docs[pl.ds(b * (CHUNK // HD) + part, 1), :]
                hot = jnp.broadcast_to(row, (HD, HD)) == r.astype(jnp.float32)
                feat[pl.ds(b, 1), part * HD:(part + 1) * HD, :] = (
                    hot.astype(jnp.float32).T.astype(jnp.bfloat16).reshape(1, HD, HD))
            return carry

        lax.fori_loop(0, 2 * NZ, body, 0)
        for s in range(2):
            hot = feat[pl.ds(s * NZ + z, 1)].reshape(CHUNK, HD).astype(jnp.float32)
            bar = ((1.0 - hot) * NEG).astype(jnp.bfloat16)
            for g in range(2):
                q[s, g, :, HD:] = bar

    head = x // 2
    my_w = pl.ds(pl.multiple_of(x * 512 + core * 256, 256), 256)
    head_cols = pl.ds(pl.multiple_of(head * HD, HD), HD)
    loads = [
        pltpu.make_async_copy(tok_ref, tok.at[x, y], loc.at[0]),
        pltpu.make_async_copy(wq_ref.at[:, my_w], wq.at[core, z * NX + x], loc.at[1]),
        pltpu.make_async_copy(wk_ref.at[:, head_cols], wkv.at[:, pl.ds(0, HD)], loc.at[2]),
        pltpu.make_async_copy(wv_ref.at[:, head_cols], wkv.at[:, pl.ds(HD, HD)], loc.at[3]),
    ]
    for load in loads:
        load.start()

    greet([at(dx=1), at(dx=2), at(dx=3), at(dy=1), at(dy=3), at(dz=1), at(dz=7), at(c=sib),
           at(dx=1, c=sib), at(dx=2, c=sib), at(dx=3, c=sib)])

    for dx in (1, 3, 2):
        cols = pl.ds(pl.multiple_of((x + dx) % NX * 512 + core * 256, 256), 256)
        put(("w", dx), wq_ref.at[:, cols], wq.at[core, z * NX + x], at(dx=dx))

    def block(u, v, h, q):
        start, size = (h * 64, 64) if q is None else (h * 64 + q * 32, 32)
        return tok.at[(x + u) % NX, (y + v) % NY, pl.ds(start, size)]

    def orient(h, a, b):
        return (a, b) if h == 0 else (b, a)

    def axis(h, order):
        return ("y", "x")[h] if order == 0 else ("x", "y")[h]

    def token_put(h, order, sign, a, b, q=None):
        d = axis(h, order) + sign
        ref = block(*orient(h, a, b), h, q)
        dz, dx, dy = step[d]
        put((d, h, a, b, q), ref, ref, at(dx=dx, dy=dy))

    def token_take(h, order, sign, a, b, q=None):
        d = axis(h, order) + sign
        move = -1 if sign == "+" else 1
        a2, b2 = (a, b + move) if order == 0 else (a + move, b)
        take((d, h, a, b, q), block(*orient(h, a2, b2), h, q))

    loads[0].wait()
    for h in (0, 1):
        for sign in "+-":
            token_put(h, 0, sign, 0, 0)
    for h in (0, 1):
        for sign in "+-":
            token_put(h, 1, sign, 0, 0)

    def ring_step(name, unit, sign, dist, h):
        way = -1 if sign == "+" else 1
        ref = unit(way * dist, h)
        if dist:
            take((name, sign, dist, h), ref)
        if dist < 3 or (dist == 3 and h == (0 if sign == "+" else 1)):
            dz = step["z" + sign][0]
            put((name, sign, dist + 1, h), ref, ref, at(dz=dz))
        if dist or sign == "+":
            put((name, "c", way * dist, h), ref, ref, at(c=sib))

    def w_unit(dz, h):
        return wq.at[core, pl.ds((z + dz) % NZ * NX + 2 * h, 2)]

    loads[1].wait()
    for dx in (1, 3, 2):
        take(("w", dx), wq.at[core, z * NX + (x - dx) % NX])
    for h in (0, 1):
        for sign in "+-":
            ring_step("W", w_unit, sign, 0, h)

    def w_round(dist, h):
        for sign in "+-":
            ring_step("W", w_unit, sign, dist, h)

    for sign, part in (("+", 0), ("-", 1)):
        for h in (0, 1):
            b = -1 if sign == "+" else 1
            token_take(h, 0, sign, 0, 0)
            token_put(h, 0, sign, 0, b, part)
            for sign2 in "+-":
                token_put(h, 1, sign2, 0, b)
    document_features()
    w_round(1, 0)
    for sign, part in (("+", 0), ("-", 1)):
        for h in (0, 1):
            token_take(h, 1, sign, 0, 0)
            token_put(h, 1, sign, -1 if sign == "+" else 1, 0, part)
    w_round(1, 1)
    for sign, part in (("+", 0), ("-", 1)):
        for h in (0, 1):
            b = -1 if sign == "+" else 1
            token_take(h, 0, sign, 0, b, part)
            for sign2 in "+-":
                token_put(h, 1, sign2, 0, 2 * b, part)
    for sign, part in (("+", 0), ("-", 1)):
        for h in (0, 1):
            token_take(h, 1, sign, -1 if sign == "+" else 1, 0, part)
    w_round(2, 0)
    for b in (-1, 1):
        for sign, part in (("+", 0), ("-", 1)):
            for h in (0, 1):
                token_take(h, 1, sign, 0, b)
                token_put(h, 1, sign, -1 if sign == "+" else 1, b, part)
        w_round(2, 1) if b == -1 else w_round(3, 0)
    for sign, part in (("+", 0), ("-", 1)):
        for h in (0, 1):
            b = -2 if sign == "+" else 2
            token_take(h, 1, sign, 0, b, part)
            token_put(h, 1, sign, -1 if sign == "+" else 1, b, part)
    for sign, part in (("+", 1), ("-", 0)):
        for h in (0, 1):
            token_take(h, 1, sign, 0, -2 if part == 0 else 2, part)
    w_round(3, 1)
    for sign, part in (("+", 0), ("-", 1)):
        a = -1 if sign == "+" else 1
        for b in (-1, 1, 2 * a):
            for h in (0, 1):
                token_take(h, 1, sign, a, b, part)

    def dot(weights, y_list):
        def body(j, carry):
            yy = y_list[0] if len(y_list) == 1 else j // 2
            col = pl.multiple_of(j % 2 * 1024, 1024)
            left = tok[:, pl.ds(yy, 1), :, pl.ds(col, 1024)].reshape(CHUNK, 1024)
            acc[...] += jnp.dot(
                left, weights(yy * 2 + j % 2), preferred_element_type=jnp.float32)
            return carry

        lax.fori_loop(0, 2 * len(y_list), body, 0)

    loads[2].wait()
    loads[3].wait()
    acc[...] = jnp.zeros_like(acc)
    dot(lambda j: wkv[pl.ds(pl.multiple_of(j * 1024, 1024), 1024), :], range(4))
    kv[pl.ds(core * NZ + z, 1)] = acc[...].astype(jnp.bfloat16).reshape(1, CHUNK, 2 * HD)

    def kv_unit(c, dz, h):
        return kv.at[c * NZ + (z + dz) % NZ, pl.ds(h * 256, 256)]

    def kv_copy(ring, dist, sign, h, ref, device):
        return pltpu.make_async_remote_copy(
            src_ref=ref, dst_ref=ref, send_sem=ksend.at[ring, dist, sign, h],
            recv_sem=krecv.at[ring, dist, sign, h], device_id=device, device_id_type=MESH)

    def kv_ring(dist, sign, h, ref):
        return kv_copy(0, dist, sign, h, ref, at(dz=1 if sign == 0 else -1))

    def kv_core(dist, sign, h, ref):
        return kv_copy(1, dist, sign, h, ref, at(c=sib))

    def behind(dist, sign):
        return -dist if sign == 0 else dist

    for h in (0, 1):
        ref = kv_unit(core, 0, h)
        for sign in (0, 1):
            kv_ring(1, sign, h, ref).start()
        kv_core(0, 0, h, ref).start()

    ring_step("W", w_unit, "+", 4, 0)
    ring_step("W", w_unit, "-", 4, 1)
    for dz in (0, -1, 1, -2, 2, -3, 3):
        for h in (0, 1):
            take(("W", "c", dz, h), wq.at[sib, pl.ds((z + dz) % NZ * NX + 2 * h, 2)])
    for dz, h in ((-4, 0), (4, 1)):
        take(("W", "c", dz, h), wq.at[sib, pl.ds((z + dz) % NZ * NX + 2 * h, 2)])

    def q_dot(c):
        acc[...] = jnp.zeros_like(acc)
        dot(lambda j: wq[pl.ds(c, 1), pl.ds(j * 4, 4)].reshape(1024, 256), range(4))
        return (acc[...] * (LOG2E / math.sqrt(HD))).astype(jnp.bfloat16)

    qsend[...] = q_dot(sib)
    put(("Q",), qsend, qland, at(c=sib))
    mine = q_dot(core)
    for g in (0, 1):
        q[pl.ds(core, 1), g, :, :HD] = mine[:, g * HD:(g + 1) * HD].reshape(1, CHUNK, HD)
    take(("Q",), qland)
    for g in (0, 1):
        q[pl.ds(sib, 1), g, :, :HD] = qland[:, g * HD:(g + 1) * HD].reshape(1, CHUNK, HD)
    for h in (0, 1):
        kv_core(0, 0, h, kv_unit(sib, 0, h)).wait_recv()

    def scores_of(piece):
        s, g, blocks = piece
        queries = q[s, g]
        found = []
        for b, diagonal in blocks:
            keys = jnp.concatenate(
                [kv[pl.ds(b, 1), :, :HD], feat[pl.ds(b, 1)]], axis=2).reshape(CHUNK, 2 * HD)
            one = lax.dot_general(
                queries, keys, (((1,), (1,)), ((), ())), preferred_element_type=jnp.float32)
            if diagonal:
                row = lax.broadcasted_iota(jnp.int32, (CHUNK, CHUNK), 0)
                key = lax.broadcasted_iota(jnp.int32, (CHUNK, CHUNK), 1)
                one = jnp.where(key <= row, one, NEG)
            found.append(one)
        return found

    def attend(pieces, fresh=False):
        ahead = scores_of(pieces[0])
        for i, (s, g, blocks) in enumerate(pieces):
            found = ahead
            if i + 1 < len(pieces):
                ahead = scores_of(pieces[i + 1])
            high = jnp.max(functools.reduce(jnp.maximum, found), axis=1, keepdims=True)
            high = jnp.broadcast_to(high, (CHUNK, HD))
            if not fresh:
                old = top[s, g]
                high = jnp.maximum(old, high)
                shrink = jnp.exp2(old - high)
            top[s, g] = high
            wide = jnp.concatenate([high] * (CHUNK // HD), axis=1)
            added = None
            for one, (b, _) in zip(found, blocks):
                weight = jnp.exp2(one - wide).astype(jnp.bfloat16)
                values = jnp.concatenate(
                    [kv[pl.ds(b, 1), :, HD:].reshape(CHUNK, HD),
                     jnp.ones((CHUNK, HD), jnp.bfloat16)], axis=1)
                part = jnp.dot(weight, values, preferred_element_type=jnp.float32)
                added = part if added is None else added + part
            if fresh:
                ctx_acc[s, g] = added
            else:
                ctx_acc[s, g] = (
                    ctx_acc[s, g] * jnp.concatenate([shrink, shrink], axis=1) + added)

    attend([(1, 0, [(z, False), (NZ + z, True)]), (1, 1, [(z, False), (NZ + z, True)]),
            (0, 0, [(z, True)]), (0, 1, [(z, True)])], fresh=True)

    def visit(other):
        earlier = other < z

        @pl.when(earlier)
        def _():
            pair = [(other, False), (NZ + other, False)]
            attend([(1, 0, pair), (1, 1, pair), (0, 0, pair[:1]), (0, 1, pair[:1])])

        @pl.when(jnp.logical_not(earlier))
        def _():
            attend([(1, 0, [(other, False)]), (1, 1, [(other, False)])])

    def kv_round(dist, carry):
        for h in (0, 1):
            for sign in (0, 1):
                ref = kv_unit(core, behind(dist, sign), h)
                kv_ring(dist, sign, h, ref).wait_recv()
                if h == sign:
                    kv_ring(dist + 1, sign, h, ref).start()
                else:
                    @pl.when(dist < 3)
                    def _():
                        kv_ring(dist + 1, sign, h, ref).start()
                kv_core(dist, sign, h, ref).start()
        for h in (0, 1):
            for sign in (0, 1):
                kv_core(dist, sign, h, kv_unit(sib, behind(dist, sign), h)).wait_recv()

        def one(sign, carry):
            visit((z + jnp.where(sign == 0, NZ - dist, dist)) % NZ)
            return carry

        lax.fori_loop(0, 2, one, 0)
        return carry

    lax.fori_loop(1, 4, kv_round, 0)

    for h in (0, 1):
        ref = kv_unit(core, 4, h)
        kv_ring(4, h, h, ref).wait_recv()
        kv_core(4, h, h, ref).start()
    for h in (0, 1):
        kv_core(4, h, h, kv_unit(sib, 4, h)).wait_recv()
    far = (z + 4) % NZ

    def finish(s):
        for g in (0, 1):
            ctx[s, :, g * HD:(g + 1) * HD] = (
                ctx_acc[s, g, :, :HD] / ctx_acc[s, g, :, HD:]).astype(jnp.bfloat16)
        cols = pl.ds(pl.multiple_of(x * 512 + core * 256, 256), 256)
        for dx in (2, 1, 3, 0):
            rows = pl.ds(pl.multiple_of((x + dx) % NX * ROWS, ROWS), ROWS)
            src, dst = ctx.at[s, rows], out_ref.at[:, cols]
            if dx:
                put_out(s, dx, src, dst)
            else:
                @pl.when(core == s)
                def _():
                    pltpu.make_async_copy(src, dst, loc.at[0]).start()

                @pl.when(core != s)
                def _():
                    put_out(s, 0, src, dst)

    def out_copy(s, dx, src, dst):
        i = 4 * core + dx
        return pltpu.make_async_remote_copy(
            src_ref=src, dst_ref=dst, send_sem=osend.at[s, dx], recv_sem=orecv.at[i],
            device_id=at(dx=dx, c=s), device_id_type=MESH)

    def put_out(s, dx, src, dst):
        out_copy(s, dx, src, dst).start()

    @pl.when(far < z)
    def _():
        attend([(0, 0, [(far, False)]), (0, 1, [(far, False)])])

    finish(0)

    @pl.when(far < z)
    def _():
        pair = [(far, False), (NZ + far, False)]
        attend([(1, 0, pair), (1, 1, pair)])

    @pl.when(far >= z)
    def _():
        attend([(1, 0, [(far, False)]), (1, 1, [(far, False)])])

    finish(1)

    def out_land(c, dx):
        return out_ref.at[:, pl.ds(pl.multiple_of((x - dx) % NX * 512 + c * 256, 256), 256)]

    def out_wait(c, dx):
        land = out_land(c, dx)
        pltpu.make_async_remote_copy(
            src_ref=land, dst_ref=land, send_sem=osend.at[0, dx], recv_sem=orecv.at[4 * c + dx],
            device_id=at(c=sib), device_id_type=MESH).wait_recv()

    for c in (0, 1):
        for dx in (1, 2, 3):
            out_wait(c, dx)
    out_wait(sib, 0)
    own = out_land(core, 0)
    pltpu.make_async_copy(own, own, loc.at[0]).wait()

    for copy in sent:
        copy.wait_send()
    piece = ctx.at[0, pl.ds(0, ROWS)]
    for s in (0, 1):
        for dx in (1, 2, 3):
            out_copy(s, dx, piece, piece).wait_send()

        @pl.when(core != s)
        def _():
            out_copy(s, 0, piece, piece).wait_send()
    for h in (0, 1):
        ref = kv_unit(core, 0, h)
        kv_core(0, 0, h, ref).wait_send()
        for sign in (0, 1):
            for dist in (1, 2, 3):
                kv_ring(dist, sign, h, ref).wait_send()
                kv_core(dist, sign, h, ref).wait_send()
        kv_ring(4, h, h, ref).wait_send()
        kv_core(4, h, h, ref).wait_send()


COPIES = 96


def local(tokens, positions, w_query, w_key, w_value):
    anywhere = pl.BlockSpec(memory_space=pltpu.HBM)
    vmem = pl.BlockSpec(memory_space=pltpu.VMEM)
    return pl.pallas_call(
        kernel_body,
        name="layer",
        out_shape=jax.ShapeDtypeStruct((ROWS, 2048), jnp.bfloat16),
        in_specs=[anywhere, vmem, anywhere, anywhere, anywhere],
        out_specs=vmem,
        scratch_shapes=[
            pltpu.VMEM((NX, NY, ROWS, 2048), jnp.bfloat16),
            pltpu.VMEM((2, NZ * NX, 256, 256), jnp.bfloat16),
            pltpu.VMEM((8192, 2 * HD), jnp.bfloat16),
            pltpu.VMEM((2 * NZ, CHUNK, 2 * HD), jnp.bfloat16),
            pltpu.VMEM((2 * NZ, CHUNK, HD), jnp.bfloat16),
            pltpu.VMEM((2, 2, CHUNK, 2 * HD), jnp.bfloat16),
            pltpu.VMEM((CHUNK, 256), jnp.bfloat16),
            pltpu.VMEM((CHUNK, 256), jnp.bfloat16),
            pltpu.VMEM((CHUNK, 256), jnp.float32),
            pltpu.VMEM((64, HD), jnp.float32),
            pltpu.VMEM((2, 2, CHUNK, HD), jnp.float32),
            pltpu.VMEM((2, 2, CHUNK, 2 * HD), jnp.float32),
            pltpu.VMEM((2, CHUNK, 256), jnp.bfloat16),
            pltpu.SemaphoreType.DMA((4,)),
            pltpu.SemaphoreType.DMA((COPIES,)),
            pltpu.SemaphoreType.DMA((COPIES,)),
            pltpu.SemaphoreType.DMA((2, 5, 2, 2)),
            pltpu.SemaphoreType.DMA((2, 5, 2, 2)),
            pltpu.SemaphoreType.DMA((2, 4)),
            pltpu.SemaphoreType.DMA((8,)),
        ],
        compiler_params=pltpu.CompilerParams(
            collective_id=0, has_side_effects=True, vmem_limit_bytes=60 * 2**20),
    )(tokens, positions.reshape(64, HD), w_query, w_key, w_value)


def solution(mesh):
    in_specs = (P(("seq", "row"), "col"), P(), P("row", "col"), P(None, "col"), P(None, "col"))
    out_specs = P(("seq", "row"), "col")
    return jax.shard_map(local, mesh=mesh, in_specs=in_specs, out_specs=out_specs, check_vma=False)
```

time: 126 us -> 111 us (0.88)
  the two profiles are of different devices: /device:TPU:96 before, /device:TPU:1 now
where the time goes in v2:
time: 111 us
  Pallas kernels  109 us (98%)
  local copies, waits for them, and re-layouts  1.88 us (2%)
    pallas_call x1, Pallas kernels, local(): pl.pallas_call(kernel_body, name='layer', out_shape=jax.ShapeDtypeStruct(...  109 us

profile of v2, /device:TPU:1, one launch (start us, length us, event | category | flops | bytes accessed | tf_op | source)
XLA Modules:
  0.0 111.2 jit_solution(17468034403723246270)
XLA Ops:
  0.0 109.3 %layer.1 = bf16[128,2048]{1,0:T(8,128)(2,1)} custom-call(bf16[128,2048]{1,0:T(8,128)(2,1)} %tok_ref.1, s32[64,128]{1,0:T(8,128)} %bitcast.1, bf16[256,2048]{1,0:T(8,128)(2,1)} %wq_ref.1, bf16[8192,256]{1,0:T(8,128)(2,1)} %wk_ref.1, bf16[8192,256]{1,0:T(8,128)(2,1)} %wv_ref.1), custom_call_target="tpu_custom_call" | custom-call | tf_op jit(solution)/shard_map/layer/pallas_call | solution.py:452
  109.3 1.9 %copy.7 = bf16[128,2048]{1,0:T(8,128)(2,1)} copy(bf16[128,2048]{1,0:T(8,128)(2,1)} %layer.1) | data formatting | bytes 1048576

commit v3 on v2

--- a/solution.py
+++ b/solution.py
@@ -15,6 +15,7 @@
 MESH = pl.DeviceIdType.MESH
 LOG2E = 1.4426950408889634
 NEG = -1e30
+ORDER = (0, 1, 3, 2)
 
 
 def place():
@@ -73,7 +74,7 @@
 
         def body(b, carry):
             for part in range(CHUNK // HD):
-                row = docs[pl.ds(b * (CHUNK // HD) + part, 1), :]
+                row = docs[pl.ds(b * NX + (x + ORDER[part]) % NX, 1), :]
                 hot = jnp.broadcast_to(row, (HD, HD)) == r.astype(jnp.float32)
                 feat[pl.ds(b, 1), part * HD:(part + 1) * HD, :] = (
                     hot.astype(jnp.float32).T.astype(jnp.bfloat16).reshape(1, HD, HD))
@@ -128,38 +129,135 @@
         take((d, h, a, b, q), block(*orient(h, a2, b2), h, q))
 
     loads[0].wait()
-    for h in (0, 1):
+    for h in (1, 0):
         for sign in "+-":
             token_put(h, 0, sign, 0, 0)
     for h in (0, 1):
         for sign in "+-":
             token_put(h, 1, sign, 0, 0)
 
-    def ring_step(name, unit, sign, dist, h):
+    def dot(dxs, rows, weights):
+        acc[rows, :] = jnp.zeros((len(dxs) * ROWS, 256), jnp.float32)
+
+        def body(j, carry):
+            col = pl.multiple_of(j % 2 * 1024, 1024)
+            left = jnp.concatenate(
+                [tok[pl.ds((x + dx) % NX, 1), pl.ds(j // 2, 1), :, pl.ds(col, 1024)].reshape(
+                    ROWS, 1024) for dx in dxs], axis=0)
+            acc[rows, :] += jnp.dot(left, weights(j), preferred_element_type=jnp.float32)
+            return carry
+
+        lax.fori_loop(0, 8, body, 0)
+        return acc[rows, :]
+
+    def group_rows(g):
+        return pl.ds((0, 128, 384)[g], (128, 256, 128)[g])
+
+    def kv_unit(c, dz, g):
+        return kv.at[c * NZ + (z + dz) % NZ, group_rows(g)]
+
+    def behind(dist, sign):
+        return -dist if sign == 0 else dist
+
+    def kv_copy(i, dist, sign, ref, device):
+        return pltpu.make_async_remote_copy(
+            src_ref=ref, dst_ref=ref, send_sem=ksend.at[i, dist, sign],
+            recv_sem=krecv.at[i, dist, sign], device_id=device, device_id_type=MESH)
+
+    def kv_ring(g, dist, sign, ref):
+        return kv_copy(0, dist, sign, ref, at(dz=1 if sign == 0 else -1))
+
+    def kv_core(g, dist, sign, ref):
+        return kv_copy(1, dist, sign, ref, at(c=sib))
+
+    def kv_half(dz, sign):
+        return kv.at[core * NZ + (z + dz) % NZ, pl.ds(128 + 128 * sign, 128)]
+
+    def kv_project(g):
+        rows = group_rows(g)
+        dxs = ((0,), (1, 3), (2,))[g]
+        found = dot(dxs, rows, lambda j: wkv[pl.ds(pl.multiple_of(j * 1024, 1024), 1024), :])
+        kv[pl.ds(core * NZ + z, 1), rows] = found.astype(jnp.bfloat16).reshape(
+            1, len(dxs) * ROWS, 2 * HD)
+        ref = kv_unit(core, 0, g)
+        for sign in (0, 1):
+            if g == 2:
+                kv_ring(2, 1, sign, ref).start()
+            else:
+                put(("K", g, 1, sign), ref, ref, at(dz=1 - 2 * sign))
+        if g == 2:
+            kv_core(2, 0, 0, ref).start()
+        else:
+            put(("K", g, "c", 0), ref, ref, at(c=sib))
+
+    def kv_event(g, dist):
+        for sign in (0, 1):
+            dz = behind(dist, sign)
+            if dist == 4:
+                if g == 0 and sign == 1:
+                    continue
+                ref = kv_unit(core, 4, 0) if g == 0 else kv_half(4, sign)
+                take(("K", g, 4, sign), ref)
+                put(("K", g, "c", 4, sign), ref, ref, at(c=sib))
+                continue
+            ref = kv_unit(core, dz, g)
+            take(("K", g, dist, sign), ref)
+            onward = ref
+            if dist == 3 and g == 1:
+                onward = kv_half(dz, sign)
+            if dist < 3 or g == 1 or sign == 0:
+                put(("K", g, dist + 1, sign), onward, onward, at(dz=1 - 2 * sign))
+            put(("K", g, "c", dz), ref, ref, at(c=sib))
+
+    def kv_core_wait(g, dz):
+        if dz == 4:
+            for sign in ((0,) if g == 0 else (0, 1)):
+                rows = group_rows(0) if g == 0 else pl.ds(128 + 128 * sign, 128)
+                take(("K", g, "c", 4, sign), kv.at[sib * NZ + (z + 4) % NZ, rows])
+        else:
+            take(("K", g, "c", dz), kv_unit(sib, dz, g))
+
+    def q_project(groups, c):
+        first = (0, 128, 384)[groups[0]]
+        dxs = sum((((0,), (1, 3), (2,))[g] for g in groups), ())
+        size = len(dxs) * ROWS
+        rows = pl.ds(first, size)
+        found = dot(dxs, rows, lambda j: wq[pl.ds(c, 1), pl.ds(j * 4, 4)].reshape(1024, 256))
+        found = (found * (LOG2E / math.sqrt(HD))).astype(jnp.bfloat16)
+        if c is sib:
+            qsend[rows, :] = found
+            part = 0 if first == 0 else 1
+            put(("Q", part), qsend.at[rows], qland.at[rows], at(c=sib))
+        else:
+            for g in (0, 1):
+                q[pl.ds(core, 1), g, rows, :HD] = found[:, g * HD:(g + 1) * HD].reshape(
+                    1, size, HD)
+
+    def ring_step(name, unit, sign, dist, r, plus):
         way = -1 if sign == "+" else 1
-        ref = unit(way * dist, h)
+        ref = unit(way * dist, r)
         if dist:
-            take((name, sign, dist, h), ref)
-        if dist < 3 or (dist == 3 and h == (0 if sign == "+" else 1)):
-            dz = step["z" + sign][0]
-            put((name, sign, dist + 1, h), ref, ref, at(dz=dz))
+            take((name, sign, dist, r), ref)
+        if dist < 3 or (dist == 3 and plus == (sign == "+")):
+            put((name, sign, dist + 1, r), ref, ref, at(dz=step["z" + sign][0]))
         if dist or sign == "+":
-            put((name, "c", way * dist, h), ref, ref, at(c=sib))
-
-    def w_unit(dz, h):
-        return wq.at[core, pl.ds((z + dz) % NZ * NX + 2 * h, 2)]
+            put((name, "c", way * dist, r), ref, ref, at(c=sib))
 
     loads[1].wait()
-    for dx in (1, 3, 2):
-        take(("w", dx), wq.at[core, z * NX + (x - dx) % NX])
-    for h in (0, 1):
+
+    def w_unit(dz, r):
+        return wq.at[core, (z + dz) % NZ * NX + (x + ORDER[r]) % NX]
+
+    def w_event(dist, r):
         for sign in "+-":
-            ring_step("W", w_unit, sign, 0, h)
-
-    def w_round(dist, h):
-        for sign in "+-":
-            ring_step("W", w_unit, sign, dist, h)
-
+            if dist < 4 or sign == ("+" if r < 2 else "-"):
+                ring_step("W", w_unit, sign, dist, r, r < 2)
+
+    w_event(0, 0)
+    for r, dx in ((1, 3), (2, 1), (3, 2)):
+        take(("w", dx), w_unit(0, r))
+        w_event(0, r)
+    w_event(1, 0)
     for sign, part in (("+", 0), ("-", 1)):
         for h in (0, 1):
             b = -1 if sign == "+" else 1
@@ -167,107 +265,97 @@
             token_put(h, 0, sign, 0, b, part)
             for sign2 in "+-":
                 token_put(h, 1, sign2, 0, b)
+    w_event(1, 1)
     document_features()
-    w_round(1, 0)
-    for sign, part in (("+", 0), ("-", 1)):
-        for h in (0, 1):
+    w_event(1, 2)
+    w_event(1, 3)
+    for h in (1, 0):
+        for sign, part in (("+", 0), ("-", 1)):
             token_take(h, 1, sign, 0, 0)
             token_put(h, 1, sign, -1 if sign == "+" else 1, 0, part)
-    w_round(1, 1)
-    for sign, part in (("+", 0), ("-", 1)):
-        for h in (0, 1):
+    w_event(2, 0)
+    for h in (0, 1):
+        for sign, part in (("+", 0), ("-", 1)):
             b = -1 if sign == "+" else 1
             token_take(h, 0, sign, 0, b, part)
-            for sign2 in "+-":
-                token_put(h, 1, sign2, 0, 2 * b, part)
+            if h == 0:
+                for sign2 in "+-":
+                    token_put(h, 1, sign2, 0, 2 * b, part)
+    w_event(2, 1)
     for sign, part in (("+", 0), ("-", 1)):
-        for h in (0, 1):
-            token_take(h, 1, sign, -1 if sign == "+" else 1, 0, part)
-    w_round(2, 0)
-    for b in (-1, 1):
-        for sign, part in (("+", 0), ("-", 1)):
-            for h in (0, 1):
+        token_take(1, 1, sign, -1 if sign == "+" else 1, 0, part)
+    loads[2].wait()
+    loads[3].wait()
+    kv_project(0)
+    w_event(2, 2)
+    w_event(2, 3)
+    for h in (1, 0):
+        for b in (-1, 1):
+            for sign, part in (("+", 0), ("-", 1)):
                 token_take(h, 1, sign, 0, b)
                 token_put(h, 1, sign, -1 if sign == "+" else 1, b, part)
-        w_round(2, 1) if b == -1 else w_round(3, 0)
+        if h == 1:
+            for sign, part in (("+", 0), ("-", 1)):
+                for sign2 in "+-":
+                    token_put(h, 1, sign2, 0, -2 if sign == "+" else 2, part)
+        w_event(3, 1 - h)
+    kv_event(0, 1)
+    w_event(3, 2)
     for sign, part in (("+", 0), ("-", 1)):
-        for h in (0, 1):
-            b = -2 if sign == "+" else 2
-            token_take(h, 1, sign, 0, b, part)
-            token_put(h, 1, sign, -1 if sign == "+" else 1, b, part)
+        b = -2 if sign == "+" else 2
+        token_take(0, 1, sign, 0, b, part)
+        token_put(0, 1, sign, -1 if sign == "+" else 1, b, part)
     for sign, part in (("+", 1), ("-", 0)):
-        for h in (0, 1):
-            token_take(h, 1, sign, 0, -2 if part == 0 else 2, part)
-    w_round(3, 1)
+        token_take(0, 1, sign, 0, -2 if part == 0 else 2, part)
+    w_event(3, 3)
+    kv_event(0, 2)
+    for sign, part in (("+", 0), ("-", 1)):
+        for b in (-1, 1):
+            token_take(1, 1, sign, -1 if sign == "+" else 1, b, part)
+    kv_project(1)
+    for sign, part in (("+", 0), ("-", 1)):
+        b = -2 if sign == "+" else 2
+        token_take(1, 1, sign, 0, b, part)
+        token_put(1, 1, sign, -1 if sign == "+" else 1, b, part)
+    kv_event(0, 3)
+    for r in range(4):
+        w_event(4, r)
+    kv_event(1, 1)
+    kv_event(0, 4)
+    for dz in (0, -1, 1, -2, 2, -3, 3, 4):
+        for r in range(4):
+            key = dz if abs(dz) < 4 else (-4 if r < 2 else 4)
+            take(("W", "c", key, r), wq.at[sib, (z + dz) % NZ * NX + (x + ORDER[r]) % NX])
+    q_project((0, 1), sib)
+    kv_event(1, 2)
+    q_project((0, 1), core)
+    kv_event(1, 3)
+    for sign, part in (("+", 1), ("-", 0)):
+        token_take(1, 1, sign, 0, -2 if part == 0 else 2, part)
     for sign, part in (("+", 0), ("-", 1)):
         a = -1 if sign == "+" else 1
-        for b in (-1, 1, 2 * a):
-            for h in (0, 1):
-                token_take(h, 1, sign, a, b, part)
-
-    def dot(weights, y_list):
-        def body(j, carry):
-            yy = y_list[0] if len(y_list) == 1 else j // 2
-            col = pl.multiple_of(j % 2 * 1024, 1024)
-            left = tok[:, pl.ds(yy, 1), :, pl.ds(col, 1024)].reshape(CHUNK, 1024)
-            acc[...] += jnp.dot(
-                left, weights(yy * 2 + j % 2), preferred_element_type=jnp.float32)
-            return carry
-
-        lax.fori_loop(0, 2 * len(y_list), body, 0)
-
-    loads[2].wait()
-    loads[3].wait()
-    acc[...] = jnp.zeros_like(acc)
-    dot(lambda j: wkv[pl.ds(pl.multiple_of(j * 1024, 1024), 1024), :], range(4))
-    kv[pl.ds(core * NZ + z, 1)] = acc[...].astype(jnp.bfloat16).reshape(1, CHUNK, 2 * HD)
-
-    def kv_unit(c, dz, h):
-        return kv.at[c * NZ + (z + dz) % NZ, pl.ds(h * 256, 256)]
-
-    def kv_copy(ring, dist, sign, h, ref, device):
-        return pltpu.make_async_remote_copy(
-            src_ref=ref, dst_ref=ref, send_sem=ksend.at[ring, dist, sign, h],
-            recv_sem=krecv.at[ring, dist, sign, h], device_id=device, device_id_type=MESH)
-
-    def kv_ring(dist, sign, h, ref):
-        return kv_copy(0, dist, sign, h, ref, at(dz=1 if sign == 0 else -1))
-
-    def kv_core(dist, sign, h, ref):
-        return kv_copy(1, dist, sign, h, ref, at(c=sib))
-
-    def behind(dist, sign):
-        return -dist if sign == 0 else dist
-
-    for h in (0, 1):
-        ref = kv_unit(core, 0, h)
-        for sign in (0, 1):
-            kv_ring(1, sign, h, ref).start()
-        kv_core(0, 0, h, ref).start()
-
-    ring_step("W", w_unit, "+", 4, 0)
-    ring_step("W", w_unit, "-", 4, 1)
-    for dz in (0, -1, 1, -2, 2, -3, 3):
-        for h in (0, 1):
-            take(("W", "c", dz, h), wq.at[sib, pl.ds((z + dz) % NZ * NX + 2 * h, 2)])
-    for dz, h in ((-4, 0), (4, 1)):
-        take(("W", "c", dz, h), wq.at[sib, pl.ds((z + dz) % NZ * NX + 2 * h, 2)])
-
-    def q_dot(c):
-        acc[...] = jnp.zeros_like(acc)
-        dot(lambda j: wq[pl.ds(c, 1), pl.ds(j * 4, 4)].reshape(1024, 256), range(4))
-        return (acc[...] * (LOG2E / math.sqrt(HD))).astype(jnp.bfloat16)
-
-    qsend[...] = q_dot(sib)
-    put(("Q",), qsend, qland, at(c=sib))
-    mine = q_dot(core)
-    for g in (0, 1):
-        q[pl.ds(core, 1), g, :, :HD] = mine[:, g * HD:(g + 1) * HD].reshape(1, CHUNK, HD)
-    take(("Q",), qland)
+        for b in (0, -1, 1, 2 * a):
+            token_take(0, 1, sign, a, b, part)
+        token_take(1, 1, sign, a, 2 * a, part)
+    kv_project(2)
+    q_project((2,), sib)
+    q_project((2,), core)
+    kv_event(1, 4)
+    for r in (0, 1):
+        rows = pl.ds((0, 384)[r], (384, 128)[r])
+        take(("Q", r), qland.at[rows])
     for g in (0, 1):
         q[pl.ds(sib, 1), g, :, :HD] = qland[:, g * HD:(g + 1) * HD].reshape(1, CHUNK, HD)
-    for h in (0, 1):
-        kv_core(0, 0, h, kv_unit(sib, 0, h)).wait_recv()
+    for g in (0, 1):
+        for dz in (0, -1, 1, -2, 2, -3, 3, 4):
+            kv_core_wait(g, dz)
+    kv_core(2, 0, 0, kv_unit(sib, 0, 2)).wait_recv()
+
+    def places(dim):
+        size = (HD, CHUNK) if dim == 0 else (CHUNK, HD)
+        return jnp.concatenate(
+            [lax.broadcasted_iota(jnp.int32, size, dim) + (x + dx) % NX * ROWS for dx in ORDER],
+            axis=dim)
 
     def scores_of(piece):
         s, g, blocks = piece
@@ -279,9 +367,7 @@
             one = lax.dot_general(
                 queries, keys, (((1,), (1,)), ((), ())), preferred_element_type=jnp.float32)
             if diagonal:
-                row = lax.broadcasted_iota(jnp.int32, (CHUNK, CHUNK), 0)
-                key = lax.broadcasted_iota(jnp.int32, (CHUNK, CHUNK), 1)
-                one = jnp.where(key <= row, one, NEG)
+                one = jnp.where(places(1) <= places(0), one, NEG)
             found.append(one)
         return found
 
@@ -316,49 +402,45 @@
     attend([(1, 0, [(z, False), (NZ + z, True)]), (1, 1, [(z, False), (NZ + z, True)]),
             (0, 0, [(z, True)]), (0, 1, [(z, True)])], fresh=True)
 
-    def visit(other):
-        earlier = other < z
-
-        @pl.when(earlier)
+    def kv_round(dist, carry):
+        for sign in (0, 1):
+            ref = kv_unit(core, behind(dist, sign), 2)
+            kv_ring(2, dist, sign, ref).wait_recv()
+            if sign == 1:
+                kv_ring(2, dist + 1, sign, ref).start()
+            else:
+                @pl.when(dist < 3)
+                def _():
+                    kv_ring(2, dist + 1, sign, ref).start()
+            kv_core(2, dist, sign, ref).start()
+        for sign in (0, 1):
+            kv_core(2, dist, sign, kv_unit(sib, behind(dist, sign), 2)).wait_recv()
+        low, high = (z + NZ - dist) % NZ, (z + dist) % NZ
+        both = [(low, False), (high, False)]
+        first = [(1, 0, both), (1, 1, both)]
+        count = jnp.where(low < z, 1, 0) + jnp.where(high < z, 1, 0)
+
+        @pl.when(count == 0)
         def _():
-            pair = [(other, False), (NZ + other, False)]
-            attend([(1, 0, pair), (1, 1, pair), (0, 0, pair[:1]), (0, 1, pair[:1])])
-
-        @pl.when(jnp.logical_not(earlier))
+            attend(first)
+
+        @pl.when(count == 1)
         def _():
-            attend([(1, 0, [(other, False)]), (1, 1, [(other, False)])])
-
-    def kv_round(dist, carry):
-        for h in (0, 1):
-            for sign in (0, 1):
-                ref = kv_unit(core, behind(dist, sign), h)
-                kv_ring(dist, sign, h, ref).wait_recv()
-                if h == sign:
-                    kv_ring(dist + 1, sign, h, ref).start()
-                else:
-                    @pl.when(dist < 3)
-                    def _():
-                        kv_ring(dist + 1, sign, h, ref).start()
-                kv_core(dist, sign, h, ref).start()
-        for h in (0, 1):
-            for sign in (0, 1):
-                kv_core(dist, sign, h, kv_unit(sib, behind(dist, sign), h)).wait_recv()
-
-        def one(sign, carry):
-            visit((z + jnp.where(sign == 0, NZ - dist, dist)) % NZ)
-            return carry
-
-        lax.fori_loop(0, 2, one, 0)
+            one = [(jnp.where(low < z, low, high), False)]
+            attend(first + [(0, 0, one), (0, 1, one)])
+
+        @pl.when(count == 2)
+        def _():
+            attend(first + [(0, 0, both), (0, 1, both)])
+
         return carry
 
     lax.fori_loop(1, 4, kv_round, 0)
 
-    for h in (0, 1):
-        ref = kv_unit(core, 4, h)
-        kv_ring(4, h, h, ref).wait_recv()
-        kv_core(4, h, h, ref).start()
-    for h in (0, 1):
-        kv_core(4, h, h, kv_unit(sib, 4, h)).wait_recv()
+    ref = kv_unit(core, 4, 2)
+    kv_ring(2, 4, 1, ref).wait_recv()
+    kv_core(2, 4, 1, ref).start()
+    kv_core(2, 4, 1, kv_unit(sib, 4, 2)).wait_recv()
     far = (z + 4) % NZ
 
     def finish(s):
@@ -366,11 +448,10 @@
             ctx[s, :, g * HD:(g + 1) * HD] = (
                 ctx_acc[s, g, :, :HD] / ctx_acc[s, g, :, HD:]).astype(jnp.bfloat16)
         cols = pl.ds(pl.multiple_of(x * 512 + core * 256, 256), 256)
-        for dx in (2, 1, 3, 0):
-            rows = pl.ds(pl.multiple_of((x + dx) % NX * ROWS, ROWS), ROWS)
-            src, dst = ctx.at[s, rows], out_ref.at[:, cols]
-            if dx:
-                put_out(s, dx, src, dst)
+        for r in (3, 1, 2, 0):
+            src, dst = ctx.at[s, pl.ds(r * ROWS, ROWS)], out_ref.at[:, cols]
+            if r:
+                out_copy(s, ORDER[r], src, dst).start()
             else:
                 @pl.when(core == s)
                 def _():
@@ -378,31 +459,35 @@
 
                 @pl.when(core != s)
                 def _():
-                    put_out(s, 0, src, dst)
+                    out_copy(s, 0, src, dst).start()
 
     def out_copy(s, dx, src, dst):
-        i = 4 * core + dx
         return pltpu.make_async_remote_copy(
-            src_ref=src, dst_ref=dst, send_sem=osend.at[s, dx], recv_sem=orecv.at[i],
+            src_ref=src, dst_ref=dst, send_sem=osend.at[s, dx], recv_sem=orecv.at[4 * core + dx],
             device_id=at(dx=dx, c=s), device_id_type=MESH)
-
-    def put_out(s, dx, src, dst):
-        out_copy(s, dx, src, dst).start()
 
     @pl.when(far < z)
     def _():
-        attend([(0, 0, [(far, False)]), (0, 1, [(far, False)])])
-
-    finish(0)
-
-    @pl.when(far < z)
-    def _():
-        pair = [(far, False), (NZ + far, False)]
-        attend([(1, 0, pair), (1, 1, pair)])
+        one = [(far, False)]
+        attend([(0, 0, one), (0, 1, one), (1, 0, one), (1, 1, one)])
 
     @pl.when(far >= z)
     def _():
         attend([(1, 0, [(far, False)]), (1, 1, [(far, False)])])
+
+    finish(0)
+
+    def pair(i, carry):
+        two = [(NZ + 2 * i, False), (NZ + 2 * i + 1, False)]
+        attend([(1, 0, two), (1, 1, two)])
+        return carry
+
+    lax.fori_loop(0, z // 2, pair, 0)
+
+    @pl.when(z % 2 == 1)
+    def _():
+        one = [(NZ + z - 1, False)]
+        attend([(1, 0, one), (1, 1, one)])
 
     finish(1)
 
@@ -432,18 +517,17 @@
         @pl.when(core != s)
         def _():
             out_copy(s, 0, piece, piece).wait_send()
-    for h in (0, 1):
-        ref = kv_unit(core, 0, h)
-        kv_core(0, 0, h, ref).wait_send()
-        for sign in (0, 1):
-            for dist in (1, 2, 3):
-                kv_ring(dist, sign, h, ref).wait_send()
-                kv_core(dist, sign, h, ref).wait_send()
-        kv_ring(4, h, h, ref).wait_send()
-        kv_core(4, h, h, ref).wait_send()
-
-
-COPIES = 96
+    ref = kv_unit(core, 0, 2)
+    kv_core(2, 0, 0, ref).wait_send()
+    for sign in (0, 1):
+        for dist in (1, 2, 3):
+            kv_ring(2, dist, sign, ref).wait_send()
+            kv_core(2, dist, sign, ref).wait_send()
+    kv_ring(2, 4, 1, ref).wait_send()
+    kv_core(2, 4, 1, ref).wait_send()
+
+
+COPIES = 168
 
 
 def local(tokens, positions, w_query, w_key, w_value):
@@ -472,8 +556,8 @@
             pltpu.SemaphoreType.DMA((4,)),
             pltpu.SemaphoreType.DMA((COPIES,)),
             pltpu.SemaphoreType.DMA((COPIES,)),
-            pltpu.SemaphoreType.DMA((2, 5, 2, 2)),
-            pltpu.SemaphoreType.DMA((2, 5, 2, 2)),
+            pltpu.SemaphoreType.DMA((2, 5, 2)),
+            pltpu.SemaphoreType.DMA((2, 5, 2)),
             pltpu.SemaphoreType.DMA((2, 4)),
             pltpu.SemaphoreType.DMA((8,)),
         ],

time: 111 us -> 115 us (1.036)
  Pallas kernels: 109 us -> 113 us
    pallas_call x1, Pallas kernels: 109 us -> 113 us  [local(): pl.pallas_call(kernel_body, name='layer', out_shape=jax.ShapeDtypeStruct(...]
where the time goes in v3:
time: 115 us; the launch traced here: 114 us
  Pallas kernels  113 us (98%)
  local copies, waits for them, and re-layouts  1.88 us (2%)
    pallas_call x1, Pallas kernels, local(): pl.pallas_call(kernel_body, name='layer', out_shape=jax.ShapeDtypeStruct(...  113 us

profile of v3, /device:TPU:1, one launch (start us, length us, event | category | flops | bytes accessed | tf_op | source)
XLA Modules:
  0.0 114.4 jit_solution(6578677817814582106)
XLA Ops:
  0.0 112.5 %layer.1 = bf16[128,2048]{1,0:T(8,128)(2,1)} custom-call(bf16[128,2048]{1,0:T(8,128)(2,1)} %tok_ref.1, s32[64,128]{1,0:T(8,128)} %bitcast.1, bf16[256,2048]{1,0:T(8,128)(2,1)} %wq_ref.1, bf16[8192,256]{1,0:T(8,128)(2,1)} %wk_ref.1, bf16[8192,256]{1,0:T(8,128)(2,1)} %wv_ref.1), custom_call_target="tpu_custom_call" | custom-call | tf_op jit(solution)/shard_map/layer/pallas_call | solution.py:536
  112.5 1.9 %copy.7 = bf16[128,2048]{1,0:T(8,128)(2,1)} copy(bf16[128,2048]{1,0:T(8,128)(2,1)} %layer.1) | data formatting | bytes 1048576

commit v4 on v3

v4 whole, which is shorter than its diff:
```python
import functools
import math

import jax
import jax.numpy as jnp
from jax import lax
from jax.experimental import pallas as pl
from jax.experimental.pallas import tpu as pltpu
from jax.sharding import PartitionSpec as P

HD = 128
NX, NY, NZ = 4, 4, 8
ROWS = 128
CHUNK = NX * ROWS
MESH = pl.DeviceIdType.MESH
LOG2E = 1.4426950408889634
NEG = -1e30
ORDER = (0, 1, 3, 2)


def place():
    row = lax.axis_index("row")
    return lax.axis_index("seq"), row // NX, row % NX, lax.axis_index("col")


def greet(partners):
    barrier = pltpu.get_barrier_semaphore()
    for partner in partners:
        pl.semaphore_signal(barrier, inc=1, device_id=partner, device_id_type=MESH)
    pl.semaphore_wait(barrier, len(partners))

DEFER = (True, True)

PLAN = (
    "feat", ("w", 1), ("w", 3), ("W", 1, 1, 0), ("W", -1, 1, 0), ("t", 0, 0, 1, 0, 0, -1),
    ("t", 0, 0, -1, 0, 0, -1), ("w", 2), ("W", 1, 1, 2), ("W", -1, 1, 2), ("W", 1, 1, 1),
    ("W", -1, 1, 1), ("t", 1, 0, 1, 0, 0, -1), ("t", 1, 0, -1, 0, 0, -1),
    ("t", 1, 1, 1, 0, 0, -1), ("t", 1, 1, -1, 0, 0, -1), ("W", 1, 2, 0), ("W", -1, 2, 0),
    ("t", 0, 0, 1, 0, -1, 0), ("t", 0, 0, -1, 0, 1, 1), ("W", 1, 1, 3), ("W", -1, 1, 3),
    ("t", 0, 1, 1, 0, 0, -1), ("t", 0, 1, -1, 0, 0, -1), ("W", 1, 2, 2), ("W", -1, 2, 2), "kv",
    ("W", 1, 2, 1), ("W", -1, 2, 1), ("t", 0, 1, 1, 0, -1, -1), ("t", 0, 1, -1, 0, -1, -1),
    ("t", 1, 1, 1, 0, -1, -1), ("t", 1, 1, -1, 0, -1, -1), ("W", 1, 3, 0), ("W", -1, 3, 0),
    ("W", 1, 2, 3), ("W", -1, 2, 3), ("t", 0, 1, 1, 0, 1, -1), ("t", 0, 1, -1, 0, 1, -1),
    ("t", 1, 1, 1, 0, 1, -1), ("t", 1, 1, -1, 0, 1, -1), ("W", 1, 3, 2), ("W", -1, 3, 2),
    ("t", 1, 0, 1, 0, -1, 0), ("t", 1, 0, -1, 0, 1, 1), ("K", 1, 1, 0), ("K", -1, 1, 0),
    ("t", 0, 1, 1, 0, -2, 0), ("W", 1, 3, 1), ("W", -1, 3, 1), ("t", 0, 1, -1, 0, 2, 1),
    ("t", 1, 1, 1, 0, -2, 0), ("W", 1, 4, 0), ("W", -1, 3, 3), ("t", 1, 1, -1, 0, 2, 1),
    ("W", 1, 3, 3), ("W", -1, 4, 2), ("kx", 1), ("kx", 3), ("K", 1, 2, 0), ("K", -1, 2, 0),
    ("kx", 2), ("W", 1, 4, 1), ("W", -1, 4, 3), ("K", 1, 1, 2), ("K", -1, 1, 2), ("K", 1, 1, 1),
    ("K", -1, 1, 1), "q01s", ("K", 1, 3, 0), ("K", -1, 3, 0), "q01c", ("K", 1, 1, 3),
    ("K", -1, 1, 3), ("K", 1, 2, 2), ("K", -1, 2, 2), "q2s", ("K", 1, 2, 1), ("K", -1, 2, 1),
    "q2c", ("K", 1, 4, 0),
)
LATE = (
    (("K", -1, 2, 3), ("K", 1, 2, 3), ("K", -1, 3, 2), ("K", 1, 3, 2), ),
    (("K", -1, 3, 1), ("K", 1, 3, 1), ("K", -1, 3, 3), ("K", 1, 3, 3), ),
    (("K", -1, 4, 2), ),
    (("K", 1, 4, 1), ("K", -1, 4, 3), ),
)

FROM = {1: 3, 2: 1, 3: 2}


def token_moves():
    t = "t"
    moves = {}
    beside = [(t, 1, 1, s, 0, 0, -1) for s in (1, -1)]
    next_to = [(t, 1, 1, s, 0, b, -1) for s in (1, -1) for b in (1, -1)]
    for h in (0, 1):
        for s in (1, -1):
            moves[t, h, h, s, 0, 0, -1] = ()
    for h in (1, 0):
        for s in (1, -1):
            moves[t, h, 1 - h, s, 0, 0, -1] = ()
    for h in (0, 1):
        for s, p in ((1, 0), (-1, 1)):
            moves[t, h, 0, s, 0, -s, p] = ((t, h, 0, s, 0, 0, -1),)
        for s, p in ((1, 0), (-1, 1)):
            moves[t, h, 1, s, -s, 0, p] = ((t, h, 1, s, 0, 0, -1),)
        for s, p in ((1, 0), (-1, 1)):
            for s2 in (1, -1):
                moves[t, h, 1, s2, 0, -s, -1] = (
                    (t, h, 0, s, 0, 0, -1),) + tuple(beside if h and DEFER[0] else ())
        for s, p in ((1, 0), (-1, 1)):
            for b in (1, -1):
                moves[t, h, 1, s, -s, b, p] = ((t, h, 1, s, 0, b, -1),)
        for s, p in ((1, 0), (-1, 1)):
            for s2 in (1, -1):
                moves[t, h, 1, s2, 0, -2 * s, p] = (
                    (t, h, 0, s, 0, -s, p),) + tuple(next_to if h and DEFER[1] else ())
        for s, p in ((1, 0), (-1, 1)):
            moves[t, h, 1, s, -s, -2 * s, p] = ((t, h, 1, s, 0, -2 * s, p),)
    return moves


def ring_moves(name, first):
    moves = {}
    for r in range(4):
        for s in (1, -1):
            moves[name, s, 1, r] = first[r]
        moves[name + "c", 0, r] = first[r]
    for dist in (1, 2, 3, 4):
        for r in range(4):
            for s in (1, -1):
                if dist < 3 or (dist == 3 and s == (1 if r < 2 else -1)):
                    moves[name, s, dist + 1, r] = ((name, s, dist, r),)
                if dist < 4 or s == (1 if r < 2 else -1):
                    moves[name + "c", -s * dist, r] = ((name, s, dist, r),)
    return moves


def all_moves():
    moves = {("w", dx): () for dx in (1, 3, 2)}
    moves.update(token_moves())
    moves.update(ring_moves("W", [()] + [(("w", FROM[r]),) for r in (1, 2, 3)]))
    moves.update({("kx", dx): ("kv",) for dx in (1, 3, 2)})
    moves.update(ring_moves("K", [("kv",)] + [(("kx", FROM[r]),) for r in (1, 2, 3)]))
    return moves


def kernel_body(
    tok_ref, pos_ref, wq_ref, wk_ref, wv_ref, out_ref, tok, wq, wkv, kvacc, kvown, kv, feat, q, qsend, qland, acc,
    docs, top, ctx_acc, ctx, loc, ssem, rsem,
    qsem, osend, orecv
):
    core, z, x, y = place()
    sib = 1 - core

    def at(dz=0, dx=0, dy=0, c=core):
        return (c, (z + dz) % NZ * NX + (x + dx) % NX, (y + dy) % NY)

    moves = all_moves()
    slots = {key: i for i, key in enumerate(moves)}
    done, sent = set(), set()

    def block(h, a, b, part):
        u, v = (a, b) if h == 0 else (b, a)
        start, size = (h * 64, 64) if part < 0 else (h * 64 + part * 32, 32)
        return tok.at[(x + u) % NX, (y + v) % NY, pl.ds(start, size)]

    def w_unit(dz, r, c=core):
        return wq.at[c, (z + dz) % NZ * NX + (x + ORDER[r]) % NX]

    def kv_unit(dz, r, c=core):
        return kv.at[c * NZ + (z + dz) % NZ, pl.ds(r * ROWS, ROWS)]

    def ends(key):
        kind = key[0]
        if kind == "t":
            _, h, order, s, a, b, part = key
            src = block(h, a, b, part)
            land = block(h, a, b - s, part) if order == 0 else block(h, a - s, b, part)
            return src, src, at(dy=s) if h == order else at(dx=s), land
        if kind == "w":
            dx = key[1]
            cols = pl.ds(pl.multiple_of((x + dx) % NX * 512 + core * 256, 256), 256)
            return wq_ref.at[:, cols], w_unit(0, 0), at(dx=dx), w_unit(0, ORDER.index(NX - dx))
        if kind == "kx":
            dx = key[1]
            land = kv_unit(0, ORDER.index(NX - dx))
            return kvown.at[(x + dx) % NX // 2], land, at(dx=dx), land
        unit = w_unit if kind[0] == "W" else kv_unit
        if kind[1:] == "c":
            src = unit(key[1], key[2])
            return src, src, at(c=sib), unit(key[1], key[2], sib)
        _, s, dist, r = key
        src = unit(-s * (dist - 1), r)
        return src, src, at(dz=s), unit(-s * dist, r)

    def copy_of(key):
        src, dst, device, _ = ends(key)
        i = slots[key]
        return pltpu.make_async_remote_copy(
            src_ref=src, dst_ref=dst, send_sem=ssem.at[i], recv_sem=rsem.at[i],
            device_id=device, device_id_type=MESH)

    def fire():
        for key, needs in moves.items():
            if key not in sent and all(need in done for need in needs):
                sent.add(key)
                copy_of(key).start()

    def take(key):
        if key in done:
            return
        land = ends(key)[3]
        i = slots[key]
        pltpu.make_async_remote_copy(
            src_ref=land, dst_ref=land, send_sem=ssem.at[i], recv_sem=rsem.at[i],
            device_id=at(c=sib), device_id_type=MESH).wait_recv()
        done.add(key)
        fire()

    def take_tokens(offsets):
        for key in moves:
            if key[0] == "t":
                _, h, order, s, a, b, _ = key
                a, b = (a, b - s) if order == 0 else (a - s, b)
                if (a if h == 0 else b) % NX in offsets:
                    take(key)

    def document_features():
        first = (pos_ref[...] == 0).astype(jnp.bfloat16)
        r = lax.broadcasted_iota(jnp.int32, (HD, HD), 0)
        c = lax.broadcasted_iota(jnp.int32, (HD, HD), 1)
        within = jnp.dot(first, (r <= c).astype(jnp.bfloat16), preferred_element_type=jnp.float32)
        total = jnp.broadcast_to(within[:, HD - 1:], within.shape).astype(jnp.bfloat16)
        before = (c < r).astype(jnp.bfloat16)[:64, :64]
        docs[...] = within + jnp.dot(before, total, preferred_element_type=jnp.float32)

        def body(b, carry):
            for part in range(CHUNK // HD):
                row = docs[pl.ds(b * NX + (x + ORDER[part]) % NX, 1), :]
                hot = jnp.broadcast_to(row, (HD, HD)) == r.astype(jnp.float32)
                feat[pl.ds(b, 1), part * HD:(part + 1) * HD, :] = (
                    hot.astype(jnp.float32).T.astype(jnp.bfloat16).reshape(1, HD, HD))
            return carry

        lax.fori_loop(0, 2 * NZ, body, 0)
        for s in range(2):
            hot = feat[pl.ds(s * NZ + z, 1)].reshape(CHUNK, HD).astype(jnp.float32)
            bar = ((1.0 - hot) * NEG).astype(jnp.bfloat16)
            for g in range(2):
                q[s, g, :, HD:] = bar

    my_w = pl.ds(pl.multiple_of(x * 512 + core * 256, 256), 256)
    loads = [
        pltpu.make_async_copy(tok_ref, tok.at[x, y], loc.at[0]),
        pltpu.make_async_copy(wq_ref.at[:, my_w], wq.at[core, z * NX + x], loc.at[1]),
    ]
    for i in range(4):
        source = (wk_ref, wv_ref)[i % 2].at[:, pl.ds(i // 2 * HD, HD)]
        loads.append(pltpu.make_async_copy(source, wkv.at[:, pl.ds(i * HD, HD)], loc.at[2 + i]))
    for load in loads:
        load.start()

    greet([at(dx=1), at(dx=2), at(dx=3), at(dy=1), at(dy=3), at(dz=1), at(dz=7), at(c=sib),
           at(dx=1, c=sib), at(dx=2, c=sib), at(dx=3, c=sib)])

    loads[0].wait()
    loads[1].wait()
    fire()

    def dot(dxs, rows, weights):
        acc[rows, :] = jnp.zeros((len(dxs) * ROWS, 256), jnp.float32)

        def body(j, carry):
            col = pl.multiple_of(j % 2 * 1024, 1024)
            left = jnp.concatenate(
                [tok[pl.ds((x + dx) % NX, 1), pl.ds(j // 2, 1), :, pl.ds(col, 1024)].reshape(
                    ROWS, 1024) for dx in dxs], axis=0)
            acc[rows, :] += jnp.dot(left, weights(j), preferred_element_type=jnp.float32)
            return carry

        lax.fori_loop(0, 8, body, 0)
        return acc[rows, :]

    def kv_project():
        kvacc[...] = jnp.zeros_like(kvacc)

        def body(j, carry):
            left = tok[pl.ds(x, 1), pl.ds(j // 2, 1), :,
                       pl.ds(pl.multiple_of(j % 2 * 1024, 1024), 1024)].reshape(ROWS, 1024)
            kvacc[...] += jnp.dot(
                left, wkv[pl.ds(pl.multiple_of(j * 1024, 1024), 1024), :],
                preferred_element_type=jnp.float32)
            return carry

        lax.fori_loop(0, 8, body, 0)
        for head in (0, 1):
            kvown[head] = kvacc[:, head * 256:head * 256 + 256].astype(jnp.bfloat16)
        kv[pl.ds(core * NZ + z, 1), 0:ROWS] = kvown[pl.ds(x // 2, 1)]

    def q_copy(i):
        rows = pl.ds((0, 384)[i], (384, 128)[i])
        return pltpu.make_async_remote_copy(
            src_ref=qsend.at[rows], dst_ref=qland.at[rows], send_sem=qsem.at[0, i],
            recv_sem=qsem.at[1, i], device_id=at(c=sib), device_id_type=MESH)

    def q_project(groups, c):
        first = (0, 128, 384)[groups[0]]
        dxs = sum((((0,), (1, 3), (2,))[g] for g in groups), ())
        size = len(dxs) * ROWS
        rows = pl.ds(first, size)
        found = dot(dxs, rows, lambda j: wq[pl.ds(c, 1), pl.ds(j * 4, 4)].reshape(1024, 256))
        found = (found * (LOG2E / math.sqrt(HD))).astype(jnp.bfloat16)
        if c is sib:
            qsend[rows, :] = found
            q_copy(0 if first == 0 else 1).start()
        else:
            for g in (0, 1):
                q[pl.ds(core, 1), g, rows, :HD] = found[:, g * HD:(g + 1) * HD].reshape(
                    1, size, HD)

    def ring_step(name, unit, sign, dist, r, plus):
        way = -1 if sign == "+" else 1
        ref = unit(way * dist, r)
        if dist:
            take((name, sign, dist, r), ref)
        if dist < 3 or (dist == 3 and plus == (sign == "+")):
            put((name, sign, dist + 1, r), ref, ref, at(dz=step["z" + sign][0]))
        if dist or sign == "+":
            put((name, "c", way * dist, r), ref, ref, at(c=sib))

    def kv_core_wait(dist):
        for key in moves:
            if key[0] == "Kc" and abs(key[1]) == dist:
                take(key)

    for entry in PLAN:
        if entry == "feat":
            document_features()
        elif entry == "kv":
            take_tokens((0,))
            for load in loads[2:]:
                load.wait()
            kv_project()
            done.add("kv")
            fire()
        elif entry == "q01s":
            take_tokens((0, 1, 3))
            for key in moves:
                if key[0][0] == "W":
                    take(key)
            q_project((0, 1), sib)
        elif entry == "q01c":
            q_project((0, 1), core)
        elif entry == "q2s":
            take_tokens((2,))
            q_project((2,), sib)
        elif entry == "q2c":
            q_project((2,), core)
        else:
            take(entry)
    for i in (0, 1):
        q_copy(i).wait_recv()
    for g in (0, 1):
        q[pl.ds(sib, 1), g, :, :HD] = qland[:, g * HD:(g + 1) * HD].reshape(1, CHUNK, HD)
    kv_core_wait(0)

    def places(dim):
        size = (HD, CHUNK) if dim == 0 else (CHUNK, HD)
        return jnp.concatenate(
            [lax.broadcasted_iota(jnp.int32, size, dim) + (x + dx) % NX * ROWS for dx in ORDER],
            axis=dim)

    def scores_of(piece):
        s, g, blocks = piece
        queries = q[s, g]
        found = []
        for b, diagonal in blocks:
            keys = jnp.concatenate(
                [kv[pl.ds(b, 1), :, :HD], feat[pl.ds(b, 1)]], axis=2).reshape(CHUNK, 2 * HD)
            one = lax.dot_general(
                queries, keys, (((1,), (1,)), ((), ())), preferred_element_type=jnp.float32)
            if diagonal:
                one = jnp.where(places(1) <= places(0), one, NEG)
            found.append(one)
        return found

    def attend(pieces, fresh=False):
        ahead = scores_of(pieces[0])
        for i, (s, g, blocks) in enumerate(pieces):
            found = ahead
            if i + 1 < len(pieces):
                ahead = scores_of(pieces[i + 1])
            high = jnp.max(functools.reduce(jnp.maximum, found), axis=1, keepdims=True)
            high = jnp.broadcast_to(high, (CHUNK, HD))
            if not fresh:
                old = top[s, g]
                high = jnp.maximum(old, high)
                shrink = jnp.exp2(old - high)
            top[s, g] = high
            wide = jnp.concatenate([high] * (CHUNK // HD), axis=1)
            added = None
            for one, (b, _) in zip(found, blocks):
                weight = jnp.exp2(one - wide).astype(jnp.bfloat16)
                values = jnp.concatenate(
                    [kv[pl.ds(b, 1), :, HD:].reshape(CHUNK, HD),
                     jnp.ones((CHUNK, HD), jnp.bfloat16)], axis=1)
                part = jnp.dot(weight, values, preferred_element_type=jnp.float32)
                added = part if added is None else added + part
            if fresh:
                ctx_acc[s, g] = added
            else:
                ctx_acc[s, g] = (
                    ctx_acc[s, g] * jnp.concatenate([shrink, shrink], axis=1) + added)

    def finish(s):
        for g in (0, 1):
            ctx[s, :, g * HD:(g + 1) * HD] = (
                ctx_acc[s, g, :, :HD] / ctx_acc[s, g, :, HD:]).astype(jnp.bfloat16)
        cols = pl.ds(pl.multiple_of(x * 512 + core * 256, 256), 256)
        for r in (3, 1, 2, 0):
            src, dst = ctx.at[s, pl.ds(r * ROWS, ROWS)], out_ref.at[:, cols]
            if r:
                out_copy(s, ORDER[r], src, dst).start()
            else:
                @pl.when(core == s)
                def _():
                    pltpu.make_async_copy(src, dst, loc.at[0]).start()

                @pl.when(core != s)
                def _():
                    out_copy(s, 0, src, dst).start()

    def out_copy(s, dx, src, dst):
        return pltpu.make_async_remote_copy(
            src_ref=src, dst_ref=dst, send_sem=osend.at[s, dx], recv_sem=orecv.at[4 * core + dx],
            device_id=at(dx=dx, c=s), device_id_type=MESH)

    attend([(1, 0, [(z, False), (NZ + z, True)]), (1, 1, [(z, False), (NZ + z, True)]),
            (0, 0, [(z, True)]), (0, 1, [(z, True)])], fresh=True)

    @pl.when(z == 0)
    def _():
        finish(0)

    def kv_round(dist, carry):
        for now in (1, 2, 3):
            @pl.when(dist == now)
            def _():
                for key in LATE[now - 1]:
                    take(key)
                kv_core_wait(now)

        low, high = (z + NZ - dist) % NZ, (z + dist) % NZ
        both = [(low, False), (high, False)]
        first = [(1, 0, both), (1, 1, both)]
        count = jnp.where(low < z, 1, 0) + jnp.where(high < z, 1, 0)

        @pl.when(count == 0)
        def _():
            attend(first)

        @pl.when(count == 1)
        def _():
            one = [(jnp.where(low < z, low, high), False)]
            attend(first + [(0, 0, one), (0, 1, one)])

        @pl.when(count == 2)
        def _():
            attend(first + [(0, 0, both), (0, 1, both)])

        @pl.when(dist == z)
        def _():
            finish(0)

        return carry

    lax.fori_loop(1, 4, kv_round, 0)

    for key in LATE[3]:
        take(key)
    kv_core_wait(4)
    far = (z + 4) % NZ

    @pl.when(far < z)
    def _():
        one = [(far, False)]
        attend([(0, 0, one), (0, 1, one), (1, 0, one), (1, 1, one)])

    @pl.when(far >= z)
    def _():
        attend([(1, 0, [(far, False)]), (1, 1, [(far, False)])])

    @pl.when(z > 3)
    def _():
        finish(0)

    def pair(i, carry):
        two = [(NZ + 2 * i, False), (NZ + 2 * i + 1, False)]
        attend([(1, 0, two), (1, 1, two)])
        return carry

    lax.fori_loop(0, z // 2, pair, 0)

    @pl.when(z % 2 == 1)
    def _():
        one = [(NZ + z - 1, False)]
        attend([(1, 0, one), (1, 1, one)])

    finish(1)

    def out_land(c, dx):
        return out_ref.at[:, pl.ds(pl.multiple_of((x - dx) % NX * 512 + c * 256, 256), 256)]

    def out_wait(c, dx):
        land = out_land(c, dx)
        pltpu.make_async_remote_copy(
            src_ref=land, dst_ref=land, send_sem=osend.at[0, dx], recv_sem=orecv.at[4 * c + dx],
            device_id=at(c=sib), device_id_type=MESH).wait_recv()

    for c in (0, 1):
        for dx in (1, 2, 3):
            out_wait(c, dx)
    out_wait(sib, 0)
    own = out_land(core, 0)
    pltpu.make_async_copy(own, own, loc.at[0]).wait()

    for key in moves:
        copy_of(key).wait_send()
    for i in (0, 1):
        q_copy(i).wait_send()
    piece = ctx.at[0, pl.ds(0, ROWS)]
    for s in (0, 1):
        for dx in (1, 2, 3):
            out_copy(s, dx, piece, piece).wait_send()

        @pl.when(core != s)
        def _():
            out_copy(s, 0, piece, piece).wait_send()


COPIES = 192


def local(tokens, positions, w_query, w_key, w_value):
    anywhere = pl.BlockSpec(memory_space=pltpu.HBM)
    vmem = pl.BlockSpec(memory_space=pltpu.VMEM)
    return pl.pallas_call(
        kernel_body,
        name="layer",
        out_shape=jax.ShapeDtypeStruct((ROWS, 2048), jnp.bfloat16),
        in_specs=[anywhere, vmem, anywhere, anywhere, anywhere],
        out_specs=vmem,
        scratch_shapes=[
            pltpu.VMEM((NX, NY, ROWS, 2048), jnp.bfloat16),
            pltpu.VMEM((2, NZ * NX, 256, 256), jnp.bfloat16),
            pltpu.VMEM((8192, 4 * HD), jnp.bfloat16),
            pltpu.VMEM((ROWS, 4 * HD), jnp.float32),
            pltpu.VMEM((2, ROWS, 2 * HD), jnp.bfloat16),
            pltpu.VMEM((2 * NZ, CHUNK, 2 * HD), jnp.bfloat16),
            pltpu.VMEM((2 * NZ, CHUNK, HD), jnp.bfloat16),
            pltpu.VMEM((2, 2, CHUNK, 2 * HD), jnp.bfloat16),
            pltpu.VMEM((CHUNK, 256), jnp.bfloat16),
            pltpu.VMEM((CHUNK, 256), jnp.bfloat16),
            pltpu.VMEM((CHUNK, 256), jnp.float32),
            pltpu.VMEM((64, HD), jnp.float32),
            pltpu.VMEM((2, 2, CHUNK, HD), jnp.float32),
            pltpu.VMEM((2, 2, CHUNK, 2 * HD), jnp.float32),
            pltpu.VMEM((2, CHUNK, 256), jnp.bfloat16),
            pltpu.SemaphoreType.DMA((6,)),
            pltpu.SemaphoreType.DMA((COPIES,)),
            pltpu.SemaphoreType.DMA((COPIES,)),
            pltpu.SemaphoreType.DMA((2, 2)),
            pltpu.SemaphoreType.DMA((2, 4)),
            pltpu.SemaphoreType.DMA((8,)),
        ],
        compiler_params=pltpu.CompilerParams(
            collective_id=0, has_side_effects=True, vmem_limit_bytes=60 * 2**20),
    )(tokens, positions.reshape(64, HD), w_query, w_key, w_value)


def solution(mesh):
    in_specs = (P(("seq", "row"), "col"), P(), P("row", "col"), P(None, "col"), P(None, "col"))
    out_specs = P(("seq", "row"), "col")
    return jax.shard_map(local, mesh=mesh, in_specs=in_specs, out_specs=out_specs, check_vma=False)
```

time: 115 us -> 97.2 us (0.85)
  the two profiles are of different devices: /device:TPU:1 before, /device:TPU:227 now
where the time goes in v4:
time: 97.2 us; the launch traced here: 97 us
  Pallas kernels  95.1 us (98%)
  local copies, waits for them, and re-layouts  1.88 us (2%)
    pallas_call x1, Pallas kernels, local(): pl.pallas_call(kernel_body, name='layer', out_shape=jax.ShapeDtypeStruct(...  95.1 us

profile of v4, /device:TPU:227, one launch (start us, length us, event | category | flops | bytes accessed | tf_op | source)
XLA Modules:
  0.0 97.0 jit_solution(9416370983388252423)
XLA Ops:
  0.0 95.1 %layer.1 = bf16[128,2048]{1,0:T(8,128)(2,1)} custom-call(bf16[128,2048]{1,0:T(8,128)(2,1)} %tok_ref.1, s32[64,128]{1,0:T(8,128)} %bitcast.1, bf16[256,2048]{1,0:T(8,128)(2,1)} %wq_ref.1, bf16[8192,256]{1,0:T(8,128)(2,1)} %wk_ref.1, bf16[8192,256]{1,0:T(8,128)(2,1)} %wv_ref.1), custom_call_target="tpu_custom_call" | custom-call | tf_op jit(solution)/shard_map/layer/pallas_call | solution.py:521
  95.1 1.9 %copy.7 = bf16[128,2048]{1,0:T(8,128)(2,1)} copy(bf16[128,2048]{1,0:T(8,128)(2,1)} %layer.1) | data formatting | bytes 1048576

commit v5 on v4

--- a/solution.py
+++ b/solution.py
@@ -15,6 +15,7 @@
 MESH = pl.DeviceIdType.MESH
 LOG2E = 1.4426950408889634
 NEG = -1e30
+CUT = (1, 1, 2)
 ORDER = (0, 1, 3, 2)
 
 
@@ -34,30 +35,31 @@
 PLAN = (
     "feat", ("w", 1), ("w", 3), ("W", 1, 1, 0), ("W", -1, 1, 0), ("t", 0, 0, 1, 0, 0, -1),
     ("t", 0, 0, -1, 0, 0, -1), ("w", 2), ("W", 1, 1, 2), ("W", -1, 1, 2), ("W", 1, 1, 1),
-    ("W", -1, 1, 1), ("t", 1, 0, 1, 0, 0, -1), ("t", 1, 0, -1, 0, 0, -1),
-    ("t", 1, 1, 1, 0, 0, -1), ("t", 1, 1, -1, 0, 0, -1), ("W", 1, 2, 0), ("W", -1, 2, 0),
+    ("W", -1, 1, 1), ("t", 1, 1, 1, 0, 0, -1), ("t", 1, 1, -1, 0, 0, -1),
+    ("t", 1, 0, 1, 0, 0, -1), ("t", 1, 0, -1, 0, 0, -1), ("W", 1, 2, 0), ("W", -1, 2, 0),
     ("t", 0, 0, 1, 0, -1, 0), ("t", 0, 0, -1, 0, 1, 1), ("W", 1, 1, 3), ("W", -1, 1, 3),
     ("t", 0, 1, 1, 0, 0, -1), ("t", 0, 1, -1, 0, 0, -1), ("W", 1, 2, 2), ("W", -1, 2, 2), "kv",
-    ("W", 1, 2, 1), ("W", -1, 2, 1), ("t", 0, 1, 1, 0, -1, -1), ("t", 0, 1, -1, 0, -1, -1),
-    ("t", 1, 1, 1, 0, -1, -1), ("t", 1, 1, -1, 0, -1, -1), ("W", 1, 3, 0), ("W", -1, 3, 0),
-    ("W", 1, 2, 3), ("W", -1, 2, 3), ("t", 0, 1, 1, 0, 1, -1), ("t", 0, 1, -1, 0, 1, -1),
-    ("t", 1, 1, 1, 0, 1, -1), ("t", 1, 1, -1, 0, 1, -1), ("W", 1, 3, 2), ("W", -1, 3, 2),
-    ("t", 1, 0, 1, 0, -1, 0), ("t", 1, 0, -1, 0, 1, 1), ("K", 1, 1, 0), ("K", -1, 1, 0),
-    ("t", 0, 1, 1, 0, -2, 0), ("W", 1, 3, 1), ("W", -1, 3, 1), ("t", 0, 1, -1, 0, 2, 1),
-    ("t", 1, 1, 1, 0, -2, 0), ("W", 1, 4, 0), ("W", -1, 3, 3), ("t", 1, 1, -1, 0, 2, 1),
-    ("W", 1, 3, 3), ("W", -1, 4, 2), ("kx", 1), ("kx", 3), ("K", 1, 2, 0), ("K", -1, 2, 0),
-    ("kx", 2), ("W", 1, 4, 1), ("W", -1, 4, 3), ("K", 1, 1, 2), ("K", -1, 1, 2), ("K", 1, 1, 1),
-    ("K", -1, 1, 1), "q01s", ("K", 1, 3, 0), ("K", -1, 3, 0), "q01c", ("K", 1, 1, 3),
-    ("K", -1, 1, 3), ("K", 1, 2, 2), ("K", -1, 2, 2), "q2s", ("K", 1, 2, 1), ("K", -1, 2, 1),
-    "q2c", ("K", 1, 4, 0),
+    ("t", 0, 1, 1, 0, -1, -1), ("t", 0, 1, -1, 0, -1, -1), ("W", 1, 2, 1), ("W", -1, 2, 1),
+    ("t", 1, 1, -1, 0, -1, -1), ("t", 1, 1, 1, 0, -1, -1), ("W", 1, 3, 0), ("W", -1, 3, 0),
+    ("t", 0, 1, 1, 0, 1, -1), ("t", 0, 1, -1, 0, 1, -1), ("W", 1, 2, 3), ("W", -1, 2, 3),
+    ("t", 1, 0, -1, 0, 1, 1), ("t", 1, 1, -1, 0, 1, -1), ("t", 1, 1, 1, 0, 1, -1),
+    ("t", 1, 0, 1, 0, -1, 0), ("W", 1, 3, 2), ("W", -1, 3, 2), ("t", 0, 1, 1, 0, -2, 0),
+    ("W", 1, 3, 1), ("W", -1, 3, 1), ("t", 0, 1, -1, 0, 2, 1), ("W", 1, 4, 0), ("W", -1, 3, 3),
+    ("t", 1, 1, -1, 0, 2, 1), ("kx", 1), ("kx", 3), ("W", 1, 3, 3), ("W", -1, 4, 2),
+    ("W", 1, 4, 1), ("W", -1, 4, 3), ("kx", 2), ("K", 1, 1, 0), ("K", -1, 1, 0),
+    ("t", 1, 1, 1, 0, -2, 0), ("K", 1, 1, 1), ("K", -1, 1, 1), "q01s", ("K", 1, 1, 2),
+    ("K", -1, 1, 2), ("K", 1, 1, 3), ("K", -1, 1, 3), "q01c", ("K", 1, 2, 0), ("K", -1, 2, 0),
+    ("K", 1, 2, 1), ("K", -1, 2, 1), "q2s", ("K", 1, 2, 2), ("K", -1, 2, 2),
 )
 LATE = (
-    (("K", -1, 2, 3), ("K", 1, 2, 3), ("K", -1, 3, 2), ("K", 1, 3, 2), ),
-    (("K", -1, 3, 1), ("K", 1, 3, 1), ("K", -1, 3, 3), ("K", 1, 3, 3), ),
-    (("K", -1, 4, 2), ),
-    (("K", 1, 4, 1), ("K", -1, 4, 3), ),
+    (("K", 1, 2, 3), ("K", -1, 2, 3), ("K", 1, 3, 0), ("K", -1, 3, 0), ),
+    (("K", 1, 3, 1), ("K", -1, 3, 1), ("K", 1, 3, 2), ("K", -1, 3, 2), ("K", 1, 3, 3), ("K", -1, 3, 3), ),
+    (("K", 1, 4, 0), ("K", 1, 4, 1), ("K", -1, 4, 2), ("K", -1, 4, 3), ),
+    (),
 )
 
+COLUMNS = {(0, -1): (0, 896), (0, 0): (0, 384), (0, 1): (384, 512),
+           (1, -1): (896, 1152), (1, 0): (896, 640), (1, 1): (1536, 512)}
 FROM = {1: 3, 2: 1, 3: 2}
 
 
@@ -111,10 +113,12 @@
 
 def all_moves():
     moves = {("w", dx): () for dx in (1, 3, 2)}
+    moves.update({("kx", dx): ("kv",) for dx in (1, 3, 2)})
     moves.update(token_moves())
     moves.update(ring_moves("W", [()] + [(("w", FROM[r]),) for r in (1, 2, 3)]))
-    moves.update({("kx", dx): ("kv",) for dx in (1, 3, 2)})
-    moves.update(ring_moves("K", [("kv",)] + [(("kx", FROM[r]),) for r in (1, 2, 3)]))
+    after = tuple(("W", s, 3, r) for s in (1, -1) for r in range(4))
+    moves.update(ring_moves(
+        "K", [("kv",) + after] + [(("kx", FROM[r]),) + after for r in (1, 2, 3)]))
     return moves
 
 
@@ -135,8 +139,8 @@
 
     def block(h, a, b, part):
         u, v = (a, b) if h == 0 else (b, a)
-        start, size = (h * 64, 64) if part < 0 else (h * 64 + part * 32, 32)
-        return tok.at[(x + u) % NX, (y + v) % NY, pl.ds(start, size)]
+        start, size = COLUMNS[h, part]
+        return tok.at[(x + u) % NX, (y + v) % NY, :, pl.ds(start, size)]
 
     def w_unit(dz, r, c=core):
         return wq.at[c, (z + dz) % NZ * NX + (x + ORDER[r]) % NX]
@@ -241,32 +245,20 @@
     loads[1].wait()
     fire()
 
-    def dot(dxs, rows, weights):
-        acc[rows, :] = jnp.zeros((len(dxs) * ROWS, 256), jnp.float32)
-
-        def body(j, carry):
-            col = pl.multiple_of(j % 2 * 1024, 1024)
-            left = jnp.concatenate(
-                [tok[pl.ds((x + dx) % NX, 1), pl.ds(j // 2, 1), :, pl.ds(col, 1024)].reshape(
-                    ROWS, 1024) for dx in dxs], axis=0)
-            acc[rows, :] += jnp.dot(left, weights(j), preferred_element_type=jnp.float32)
-            return carry
-
-        lax.fori_loop(0, 8, body, 0)
-        return acc[rows, :]
+    def tokens_of(dxs, yy):
+        return jnp.concatenate(
+            [tok[pl.ds((x + dx) % NX, 1), pl.ds(yy, 1)].reshape(ROWS, 2048) for dx in dxs], axis=0)
 
     def kv_project():
         kvacc[...] = jnp.zeros_like(kvacc)
 
         def body(j, carry):
-            left = tok[pl.ds(x, 1), pl.ds(j // 2, 1), :,
-                       pl.ds(pl.multiple_of(j % 2 * 1024, 1024), 1024)].reshape(ROWS, 1024)
             kvacc[...] += jnp.dot(
-                left, wkv[pl.ds(pl.multiple_of(j * 1024, 1024), 1024), :],
+                tokens_of((0,), j), wkv[pl.ds(pl.multiple_of(j * 2048, 2048), 2048), :],
                 preferred_element_type=jnp.float32)
             return carry
 
-        lax.fori_loop(0, 8, body, 0)
+        lax.fori_loop(0, NY, body, 0)
         for head in (0, 1):
             kvown[head] = kvacc[:, head * 256:head * 256 + 256].astype(jnp.bfloat16)
         kv[pl.ds(core * NZ + z, 1), 0:ROWS] = kvown[pl.ds(x // 2, 1)]
@@ -277,30 +269,33 @@
             src_ref=qsend.at[rows], dst_ref=qland.at[rows], send_sem=qsem.at[0, i],
             recv_sem=qsem.at[1, i], device_id=at(c=sib), device_id_type=MESH)
 
-    def q_project(groups, c):
-        first = (0, 128, 384)[groups[0]]
-        dxs = sum((((0,), (1, 3), (2,))[g] for g in groups), ())
+    def q_project(dxs, first, cores):
         size = len(dxs) * ROWS
-        rows = pl.ds(first, size)
-        found = dot(dxs, rows, lambda j: wq[pl.ds(c, 1), pl.ds(j * 4, 4)].reshape(1024, 256))
-        found = (found * (LOG2E / math.sqrt(HD))).astype(jnp.bfloat16)
-        if c is sib:
-            qsend[rows, :] = found
+        rows, width = pl.ds(first, size), pl.ds(0, 256 * len(cores))
+        acc[rows, width] = jnp.zeros((size, 256 * len(cores)), jnp.float32)
+
+        def body(j, carry):
+            weights = [wq[pl.ds(c, 1), pl.ds(j * 8, 8)].reshape(2048, 256) for c in cores]
+            acc[rows, width] += jnp.dot(
+                tokens_of(dxs, j), jnp.concatenate(weights, axis=1),
+                preferred_element_type=jnp.float32)
+            return carry
+
+        lax.fori_loop(0, NY, body, 0)
+
+        def columns(c):
+            start = pl.multiple_of(c * 256, 256) if len(cores) == 2 else 0
+            found = acc[rows, pl.ds(start, 256)]
+            return (found * (LOG2E / math.sqrt(HD))).astype(jnp.bfloat16)
+
+        if len(cores) == 2 or cores[0] is sib:
+            qsend[rows, :] = columns(sib)
             q_copy(0 if first == 0 else 1).start()
-        else:
+        if len(cores) == 2 or cores[0] is core:
+            found = columns(core)
             for g in (0, 1):
                 q[pl.ds(core, 1), g, rows, :HD] = found[:, g * HD:(g + 1) * HD].reshape(
                     1, size, HD)
-
-    def ring_step(name, unit, sign, dist, r, plus):
-        way = -1 if sign == "+" else 1
-        ref = unit(way * dist, r)
-        if dist:
-            take((name, sign, dist, r), ref)
-        if dist < 3 or (dist == 3 and plus == (sign == "+")):
-            put((name, sign, dist + 1, r), ref, ref, at(dz=step["z" + sign][0]))
-        if dist or sign == "+":
-            put((name, "c", way * dist, r), ref, ref, at(c=sib))
 
     def kv_core_wait(dist):
         for key in moves:
@@ -322,14 +317,12 @@
             for key in moves:
                 if key[0][0] == "W":
                     take(key)
-            q_project((0, 1), sib)
+            q_project((0, 1, 3), 0, (sib,))
         elif entry == "q01c":
-            q_project((0, 1), core)
+            q_project((0, 1, 3), 0, (core,))
         elif entry == "q2s":
             take_tokens((2,))
-            q_project((2,), sib)
-        elif entry == "q2c":
-            q_project((2,), core)
+            q_project((2,), 384, (0, 1))
         else:
             take(entry)
     for i in (0, 1):
@@ -345,8 +338,8 @@
             axis=dim)
 
     def scores_of(piece):
-        s, g, blocks = piece
-        queries = q[s, g]
+        s, g, blocks, rows = piece
+        queries = q[s, g, rows, :]
         found = []
         for b, diagonal in blocks:
             keys = jnp.concatenate(
@@ -358,19 +351,21 @@
             found.append(one)
         return found
 
-    def attend(pieces, fresh=False):
+    def attend(pieces, fresh=False, cut=1):
+        size = CHUNK // cut
+        pieces = [p + (pl.ds(i * size, size),) for p in pieces for i in range(cut)]
         ahead = scores_of(pieces[0])
-        for i, (s, g, blocks) in enumerate(pieces):
+        for i, (s, g, blocks, rows) in enumerate(pieces):
             found = ahead
             if i + 1 < len(pieces):
                 ahead = scores_of(pieces[i + 1])
             high = jnp.max(functools.reduce(jnp.maximum, found), axis=1, keepdims=True)
-            high = jnp.broadcast_to(high, (CHUNK, HD))
+            high = jnp.broadcast_to(high, (size, HD))
             if not fresh:
-                old = top[s, g]
+                old = top[s, g, rows, :]
                 high = jnp.maximum(old, high)
                 shrink = jnp.exp2(old - high)
-            top[s, g] = high
+            top[s, g, rows, :] = high
             wide = jnp.concatenate([high] * (CHUNK // HD), axis=1)
             added = None
             for one, (b, _) in zip(found, blocks):
@@ -380,11 +375,9 @@
                      jnp.ones((CHUNK, HD), jnp.bfloat16)], axis=1)
                 part = jnp.dot(weight, values, preferred_element_type=jnp.float32)
                 added = part if added is None else added + part
-            if fresh:
-                ctx_acc[s, g] = added
-            else:
-                ctx_acc[s, g] = (
-                    ctx_acc[s, g] * jnp.concatenate([shrink, shrink], axis=1) + added)
+            if not fresh:
+                added += ctx_acc[s, g, rows, :] * jnp.concatenate([shrink, shrink], axis=1)
+            ctx_acc[s, g, rows, :] = added
 
     def finish(s):
         for g in (0, 1):
@@ -426,21 +419,23 @@
 
         low, high = (z + NZ - dist) % NZ, (z + dist) % NZ
         both = [(low, False), (high, False)]
-        first = [(1, 0, both), (1, 1, both)]
         count = jnp.where(low < z, 1, 0) + jnp.where(high < z, 1, 0)
 
         @pl.when(count == 0)
         def _():
-            attend(first)
+            attend([(1, 0, both), (1, 1, both)], cut=CUT[0])
 
         @pl.when(count == 1)
         def _():
-            one = [(jnp.where(low < z, low, high), False)]
-            attend(first + [(0, 0, one), (0, 1, one)])
+            one = jnp.where(low < z, low, high)
+            three = both + [(NZ + one, False)]
+            attend([(1, 0, three), (1, 1, three),
+                    (0, 0, [(one, False)]), (0, 1, [(one, False)])], cut=CUT[1])
 
         @pl.when(count == 2)
         def _():
-            attend(first + [(0, 0, both), (0, 1, both)])
+            four = both + [(NZ + low, False), (NZ + high, False)]
+            attend([(1, 0, four), (1, 1, four), (0, 0, both), (0, 1, both)], cut=CUT[2])
 
         @pl.when(dist == z)
         def _():
@@ -457,28 +452,14 @@
 
     @pl.when(far < z)
     def _():
-        one = [(far, False)]
-        attend([(0, 0, one), (0, 1, one), (1, 0, one), (1, 1, one)])
+        attend([(0, 0, [(far, False)]), (0, 1, [(far, False)])])
+        finish(0)
+        two = [(far, False), (NZ + far, False)]
+        attend([(1, 0, two), (1, 1, two)])
 
     @pl.when(far >= z)
     def _():
         attend([(1, 0, [(far, False)]), (1, 1, [(far, False)])])
-
-    @pl.when(z > 3)
-    def _():
-        finish(0)
-
-    def pair(i, carry):
-        two = [(NZ + 2 * i, False), (NZ + 2 * i + 1, False)]
-        attend([(1, 0, two), (1, 1, two)])
-        return carry
-
-    lax.fori_loop(0, z // 2, pair, 0)
-
-    @pl.when(z % 2 == 1)
-    def _():
-        one = [(NZ + z - 1, False)]
-        attend([(1, 0, one), (1, 1, one)])
 
     finish(1)
 
@@ -535,7 +516,7 @@
             pltpu.VMEM((2, 2, CHUNK, 2 * HD), jnp.bfloat16),
             pltpu.VMEM((CHUNK, 256), jnp.bfloat16),
             pltpu.VMEM((CHUNK, 256), jnp.bfloat16),
-            pltpu.VMEM((CHUNK, 256), jnp.float32),
+            pltpu.VMEM((CHUNK, 512), jnp.float32),
             pltpu.VMEM((64, HD), jnp.float32),
             pltpu.VMEM((2, 2, CHUNK, HD), jnp.float32),
             pltpu.VMEM((2, 2, CHUNK, 2 * HD), jnp.float32),

time: 97.2 us -> 90.7 us (0.933)
  the two profiles are of different devices: /device:TPU:227 before, /device:TPU:1 now
where the time goes in v5:
time: 90.7 us; the launch traced here: 89.6 us
  Pallas kernels  87.7 us (97%)
  local copies, waits for them, and re-layouts  1.88 us (2%)
    pallas_call x1, Pallas kernels, local(): pl.pallas_call(kernel_body, name='layer', out_shape=jax.ShapeDtypeStruct(...  87.7 us
    unnamed x1, local copies, waits for them, and re-layouts  1.88 us

profile of v5, /device:TPU:1, one launch (start us, length us, event | category | flops | bytes accessed | tf_op | source)
XLA Modules:
  0.0 89.6 jit_solution(1878359093648788340)
XLA Ops:
  0.0 87.7 %layer.1 = bf16[128,2048]{1,0:T(8,128)(2,1)} custom-call(bf16[128,2048]{1,0:T(8,128)(2,1)} %tok_ref.1, s32[64,128]{1,0:T(8,128)} %bitcast.1, bf16[256,2048]{1,0:T(8,128)(2,1)} %wq_ref.1, bf16[8192,256]{1,0:T(8,128)(2,1)} %wk_ref.1, bf16[8192,256]{1,0:T(8,128)(2,1)} %wv_ref.1), custom_call_target="tpu_custom_call" | custom-call | tf_op jit(solution)/shard_map/layer/pallas_call | solution.py:502
  87.7 1.9 %copy.7 = bf16[128,2048]{1,0:T(8,128)(2,1)} copy(bf16[128,2048]{1,0:T(8,128)(2,1)} %layer.1) | data formatting | bytes 1048576

commit v6 on v5

--- a/solution.py
+++ b/solution.py
@@ -40,21 +40,21 @@
     ("t", 0, 0, 1, 0, -1, 0), ("t", 0, 0, -1, 0, 1, 1), ("W", 1, 1, 3), ("W", -1, 1, 3),
     ("t", 0, 1, 1, 0, 0, -1), ("t", 0, 1, -1, 0, 0, -1), ("W", 1, 2, 2), ("W", -1, 2, 2), "kv",
     ("t", 0, 1, 1, 0, -1, -1), ("t", 0, 1, -1, 0, -1, -1), ("W", 1, 2, 1), ("W", -1, 2, 1),
-    ("t", 1, 1, -1, 0, -1, -1), ("t", 1, 1, 1, 0, -1, -1), ("W", 1, 3, 0), ("W", -1, 3, 0),
-    ("t", 0, 1, 1, 0, 1, -1), ("t", 0, 1, -1, 0, 1, -1), ("W", 1, 2, 3), ("W", -1, 2, 3),
-    ("t", 1, 0, -1, 0, 1, 1), ("t", 1, 1, -1, 0, 1, -1), ("t", 1, 1, 1, 0, 1, -1),
-    ("t", 1, 0, 1, 0, -1, 0), ("W", 1, 3, 2), ("W", -1, 3, 2), ("t", 0, 1, 1, 0, -2, 0),
-    ("W", 1, 3, 1), ("W", -1, 3, 1), ("t", 0, 1, -1, 0, 2, 1), ("W", 1, 4, 0), ("W", -1, 3, 3),
-    ("t", 1, 1, -1, 0, 2, 1), ("kx", 1), ("kx", 3), ("W", 1, 3, 3), ("W", -1, 4, 2),
-    ("W", 1, 4, 1), ("W", -1, 4, 3), ("kx", 2), ("K", 1, 1, 0), ("K", -1, 1, 0),
-    ("t", 1, 1, 1, 0, -2, 0), ("K", 1, 1, 1), ("K", -1, 1, 1), "q01s", ("K", 1, 1, 2),
-    ("K", -1, 1, 2), ("K", 1, 1, 3), ("K", -1, 1, 3), "q01c", ("K", 1, 2, 0), ("K", -1, 2, 0),
-    ("K", 1, 2, 1), ("K", -1, 2, 1), "q2s", ("K", 1, 2, 2), ("K", -1, 2, 2),
+    ("t", 1, 1, -1, 0, -1, -1), ("t", 1, 1, 1, 0, -1, -1), ("t", 1, 0, -1, 0, 1, 1),
+    ("W", 1, 3, 0), ("W", -1, 3, 0), ("t", 1, 0, 1, 0, -1, 0), ("t", 0, 1, 1, 0, -2, 0),
+    ("W", 1, 2, 3), ("W", -1, 2, 3), ("t", 0, 1, -1, 0, 2, 1), ("t", 1, 1, -1, 0, 1, -1),
+    ("t", 1, 1, 1, 0, 1, -1), ("W", 1, 3, 2), ("W", -1, 3, 2), ("W", 1, 3, 1), ("W", -1, 3, 1),
+    ("kx", 1), ("kx", 3), ("W", 1, 4, 0), ("W", -1, 3, 3), ("kx", 2), ("W", 1, 3, 3),
+    ("W", -1, 4, 2), ("t", 0, 1, 1, 0, 1, -1), ("t", 0, 1, -1, 0, 1, -1),
+    ("t", 1, 1, 1, 0, -2, 0), "q01a", ("W", 1, 4, 1), ("W", -1, 4, 3), ("t", 1, 1, -1, 0, 2, 1),
+    ("K", 1, 1, 0), ("K", -1, 1, 0), ("K", 1, 1, 1), ("K", -1, 1, 1), ("K", 1, 1, 2),
+    ("K", -1, 1, 2), "q01b", ("K", 1, 1, 3), ("K", -1, 1, 3), ("K", 1, 2, 0), ("K", -1, 2, 0),
+    "q2", ("K", 1, 2, 1), ("K", -1, 2, 1),
 )
 LATE = (
-    (("K", 1, 2, 3), ("K", -1, 2, 3), ("K", 1, 3, 0), ("K", -1, 3, 0), ),
-    (("K", 1, 3, 1), ("K", -1, 3, 1), ("K", 1, 3, 2), ("K", -1, 3, 2), ("K", 1, 3, 3), ("K", -1, 3, 3), ),
-    (("K", 1, 4, 0), ("K", 1, 4, 1), ("K", -1, 4, 2), ("K", -1, 4, 3), ),
+    (("K", 1, 2, 2), ("K", -1, 2, 2), ("K", 1, 2, 3), ("K", -1, 2, 3), ),
+    (("K", 1, 3, 0), ("K", -1, 3, 0), ("K", 1, 3, 1), ("K", -1, 3, 1), ("K", 1, 3, 2), ("K", -1, 3, 2), ("K", 1, 3, 3), ("K", -1, 3, 3), ),
+    (("K", 1, 4, 0), ("K", -1, 4, 2), ("K", 1, 4, 1), ("K", -1, 4, 3), ),
     (),
 )
 
@@ -83,6 +83,8 @@
             for s2 in (1, -1):
                 moves[t, h, 1, s2, 0, -s, -1] = (
                     (t, h, 0, s, 0, 0, -1),) + tuple(beside if h and DEFER[0] else ())
+                if h == 0 and s == -1:
+                    moves[t, h, 1, s2, 0, 1, -1] += ("kv",)
         for s, p in ((1, 0), (-1, 1)):
             for b in (1, -1):
                 moves[t, h, 1, s, -s, b, p] = ((t, h, 1, s, 0, b, -1),)
@@ -269,33 +271,32 @@
             src_ref=qsend.at[rows], dst_ref=qland.at[rows], send_sem=qsem.at[0, i],
             recv_sem=qsem.at[1, i], device_id=at(c=sib), device_id_type=MESH)
 
-    def q_project(dxs, first, cores):
-        size = len(dxs) * ROWS
-        rows, width = pl.ds(first, size), pl.ds(0, 256 * len(cores))
-        acc[rows, width] = jnp.zeros((size, 256 * len(cores)), jnp.float32)
+    def q_add(dxs, first, count, start):
+        rows = pl.ds(first, len(dxs) * ROWS)
+        after = (z + 4) % NZ // 2 + 1 + start
 
         def body(j, carry):
-            weights = [wq[pl.ds(c, 1), pl.ds(j * 8, 8)].reshape(2048, 256) for c in cores]
-            acc[rows, width] += jnp.dot(
-                tokens_of(dxs, j), jnp.concatenate(weights, axis=1),
+            yy = (after + j) % NY
+            weights = [wq[c, pl.ds(yy * 8, 8)].reshape(2048, 256) for c in (0, 1)]
+            acc[rows, :] += jnp.dot(
+                tokens_of(dxs, yy), jnp.concatenate(weights, axis=1),
                 preferred_element_type=jnp.float32)
             return carry
 
-        lax.fori_loop(0, NY, body, 0)
+        lax.fori_loop(0, count, body, 0)
+
+    def q_finish(first, size):
+        rows = pl.ds(first, size)
 
         def columns(c):
-            start = pl.multiple_of(c * 256, 256) if len(cores) == 2 else 0
-            found = acc[rows, pl.ds(start, 256)]
+            found = acc[rows, pl.ds(pl.multiple_of(c * 256, 256), 256)]
             return (found * (LOG2E / math.sqrt(HD))).astype(jnp.bfloat16)
 
-        if len(cores) == 2 or cores[0] is sib:
-            qsend[rows, :] = columns(sib)
-            q_copy(0 if first == 0 else 1).start()
-        if len(cores) == 2 or cores[0] is core:
-            found = columns(core)
-            for g in (0, 1):
-                q[pl.ds(core, 1), g, rows, :HD] = found[:, g * HD:(g + 1) * HD].reshape(
-                    1, size, HD)
+        qsend[rows, :] = columns(sib)
+        q_copy(0 if first == 0 else 1).start()
+        found = columns(core)
+        for g in (0, 1):
+            q[pl.ds(core, 1), g, rows, :HD] = found[:, g * HD:(g + 1) * HD].reshape(1, size, HD)
 
     def kv_core_wait(dist):
         for key in moves:
@@ -312,17 +313,23 @@
             kv_project()
             done.add("kv")
             fire()
-        elif entry == "q01s":
+        elif entry == "q01a":
             take_tokens((0, 1, 3))
+            for key in moves:
+                if key[0] == "W" and key[2] < 4 or key[0] == "Wc" and abs(key[1]) < 4:
+                    take(key)
+            acc[...] = jnp.zeros_like(acc)
+            q_add((0, 1, 3), 0, NY - 1, 0)
+        elif entry == "q01b":
             for key in moves:
                 if key[0][0] == "W":
                     take(key)
-            q_project((0, 1, 3), 0, (sib,))
-        elif entry == "q01c":
-            q_project((0, 1, 3), 0, (core,))
-        elif entry == "q2s":
+            q_add((0, 1, 3), 0, 1, NY - 1)
+            q_finish(0, 3 * ROWS)
+        elif entry == "q2":
             take_tokens((2,))
-            q_project((2,), 384, (0, 1))
+            q_add((2,), 3 * ROWS, NY, 0)
+            q_finish(3 * ROWS, ROWS)
         else:
             take(entry)
     for i in (0, 1):

time: 90.7 us -> 90.7 us (level)
  no operation moved by 1% of the time
where the time goes in v6:
time: 90.7 us; the launch traced here: 90.1 us
  Pallas kernels  88.2 us (97%)
  local copies, waits for them, and re-layouts  1.88 us (2%)
    pallas_call x1, Pallas kernels, local(): pl.pallas_call(kernel_body, name='layer', out_shape=jax.ShapeDtypeStruct(...  88.2 us
    unnamed x1, local copies, waits for them, and re-layouts  1.88 us

profile of v6, /device:TPU:1, one launch (start us, length us, event | category | flops | bytes accessed | tf_op | source)
XLA Modules:
  0.0 90.1 jit_solution(10440685880483466609)
XLA Ops:
  0.0 88.2 %layer.1 = bf16[128,2048]{1,0:T(8,128)(2,1)} custom-call(bf16[128,2048]{1,0:T(8,128)(2,1)} %tok_ref.1, s32[64,128]{1,0:T(8,128)} %bitcast.1, bf16[256,2048]{1,0:T(8,128)(2,1)} %wq_ref.1, bf16[8192,256]{1,0:T(8,128)(2,1)} %wk_ref.1, bf16[8192,256]{1,0:T(8,128)(2,1)} %wv_ref.1), custom_call_target="tpu_custom_call" | custom-call | tf_op jit(solution)/shard_map/layer/pallas_call | solution.py:509
  88.2 1.9 %copy.7 = bf16[128,2048]{1,0:T(8,128)(2,1)} copy(bf16[128,2048]{1,0:T(8,128)(2,1)} %layer.1) | data formatting | bytes 1048576
